TPU v7x, 128 devices: a whole 4x4x4 slice. The times are simulated.
128 devices in a mesh: dp: 4 (over y), context: 8 (over z, core), tensor: 4 (over x).
Axes of the slice: x: 4, y: 4, z: 4, core: 2. Of those that a mesh axis runs over, the one named last changes fastest.
Arguments:
- tokens: bfloat16 [4, 1024, 2048], P('dp', 'context'), may hold values from -32 to 32
- routes: int32 [4, 1024, 8], P('dp', 'context'), may hold values from 0 to 63, all different within a row; in each aligned block of 128 rows (0 to 127, 128 to 255, ..., all dimensions but the last counted through in order) at most 32 rows name the same one
- attention_gain: bfloat16 [2048], P(('dp', 'context')), may hold values from 0.5 to 1.5
- query_matrix: bfloat16 [2048, 4096], P(('dp', 'context'), 'tensor'), may hold values from -0.125 to 0.125
- key_matrix: bfloat16 [2048, 512], P(('dp', 'context'), 'tensor'), may hold values from -0.125 to 0.125
- value_matrix: bfloat16 [2048, 512], P(('dp', 'context'), 'tensor'), may hold values from -0.125 to 0.125
- query_gain: bfloat16 [128], replicated, may hold values from 0.099609375 to 1.8984375
- key_gain: bfloat16 [128], replicated, may hold values from 0.099609375 to 1.8984375
- output_matrix: bfloat16 [4096, 2048], P('tensor', ('dp', 'context')), may hold values from -0.25 to 0.25
- experts_gain: bfloat16 [2048], P(('dp', 'context')), may hold values from 0.5 to 1.5
- router_matrix: bfloat16 [2048, 64], P(('dp', 'context')), may hold values from -0.0625 to 0.0625
- gate_weight: bfloat16 [64, 768, 2048], P(('dp', 'context'), 'tensor'), may hold values from -0.125 to 0.125
- up_weight: bfloat16 [64, 768, 2048], P(('dp', 'context'), 'tensor'), may hold values from -0.125 to 0.125
- down_weight: bfloat16 [64, 768, 2048], P(('dp', 'context'), 'tensor'), may hold values from -0.4375 to 0.4375
- cotangent: bfloat16 [4, 1024, 2048], P('dp', 'context'), may hold values from -10 to 10
Outputs:
- output: float32 [4, 1024, 2048], P('dp', 'context')
- tokens_grad: float32 [4, 1024, 2048], P('dp', 'context')
- attention_gain_grad: float32 [2048], P(('dp', 'context'))
- query_weight_grad: float32 [2048, 4096], P(('dp', 'context'), 'tensor')
- key_weight_grad: float32 [2048, 512], P(('dp', 'context'), 'tensor')
- value_weight_grad: float32 [2048, 512], P(('dp', 'context'), 'tensor')
- query_gain_grad: float32 [128], P(('dp', 'context'))
- key_gain_grad: float32 [128], P(('dp', 'context'))
- output_weight_grad: float32 [4096, 2048], P('tensor', ('dp', 'context'))
- experts_gain_grad: float32 [2048], P(('dp', 'context'))
- router_grad: float32 [2048, 64], P(('dp', 'context'))
- gate_grad: float32 [64, 768, 2048], P(('dp', 'context'), 'tensor')
- up_grad: float32 [64, 768, 2048], P(('dp', 'context'), 'tensor')
- down_grad: float32 [64, 768, 2048], P(('dp', 'context'), 'tensor')
Inputs may be any that keep to these rules, and one draw needn't show every extreme that they name: `routes`: each token names 8 distinct experts. In each aligned block of 128 positions of a sequence no expert is named by more than 32 tokens, and in some block one expert is named by exactly 32.
All inputs are finite; a program needn't handle non-finite values.
Results may differ from a plain program's by a relative error of at most 0.017.
Values may be sent and summed in bfloat16 or wider, within the bound.
A program may use at most 256 MiB of HBM per device.

v0:
```python
import math

import jax
import jax.numpy as jnp
from jax import lax
from jax.sharding import PartitionSpec as P

EPSILON = 1e-06
THETA = 1000000.0


def rms_parts(values, gain_vector):
    inverse = lax.rsqrt(jnp.mean(values * values, axis=-1, keepdims=True) + EPSILON)
    return (values * inverse * gain_vector, inverse)


def rms_back(values, inverse, gain_vector, grad_out):
    scaled = grad_out * gain_vector
    inner_mean = jnp.mean(scaled * values, axis=-1, keepdims=True)
    grad_in = inverse * scaled - values * (inverse * inverse * inverse) * inner_mean
    leading = tuple(range(values.ndim - 1))
    grad_gain = jnp.sum(grad_out * values * inverse, axis=leading)
    return (grad_in, grad_gain)


def rotary_tables(positions, head_size):
    half_size = head_size // 2
    frequency = jnp.exp(
        jnp.arange(half_size, dtype=jnp.float32) * (-2.0 * math.log(THETA) / head_size)
    )
    angles = positions[:, None] * frequency[None, :]
    return (jnp.cos(angles)[:, None, :], jnp.sin(angles)[:, None, :])


def rotate(values, cosine_table, sine_table):
    half_size = values.shape[-1] // 2
    first_half = values[..., :half_size]
    second_half = values[..., half_size:]
    return jnp.concatenate(
        [
            first_half * cosine_table - second_half * sine_table,
            second_half * cosine_table + first_half * sine_table,
        ],
        axis=-1,
    )


def rotate_back(grad_out, cosine_table, sine_table):
    half_size = grad_out.shape[-1] // 2
    first_half = grad_out[..., :half_size]
    second_half = grad_out[..., half_size:]
    return jnp.concatenate(
        [
            first_half * cosine_table + second_half * sine_table,
            second_half * cosine_table - first_half * sine_table,
        ],
        axis=-1,
    )


def per_device(
    tokens,
    routes,
    attention_gain,
    query_matrix,
    key_matrix,
    value_matrix,
    query_gain,
    key_gain,
    output_matrix,
    experts_gain,
    router_matrix,
    gate_weight,
    up_weight,
    down_weight,
    cotangent,
):
    sequences, block_rows, model_width = tokens.shape
    top_count = routes.shape[2]
    expert_count = router_matrix.shape[1]
    local_experts = gate_weight.shape[0]
    head_size = query_gain.shape[0]
    query_heads = query_matrix.shape[1] // head_size
    key_heads = key_matrix.shape[1] // head_size
    group_size = query_heads // key_heads
    owners = lax.axis_size(("dp", "context"))
    length = block_rows * lax.axis_size("context")
    capacity = max(2, 2 * block_rows * top_count // expert_count)
    score_scale = head_size ** (-0.5)
    gathered = (
        lax.all_gather(attention_gain, ("dp", "context"), axis=0, tiled=True),
        lax.all_gather(query_matrix, ("dp", "context"), axis=0, tiled=True),
        lax.all_gather(key_matrix, ("dp", "context"), axis=0, tiled=True),
        lax.all_gather(value_matrix, ("dp", "context"), axis=0, tiled=True),
        lax.all_gather(output_matrix, ("dp", "context"), axis=1, tiled=True),
        lax.all_gather(experts_gain, ("dp", "context"), axis=0, tiled=True),
        lax.all_gather(router_matrix, ("dp", "context"), axis=0, tiled=True),
    )
    first_gain = gathered[0].astype(jnp.float32)
    query_full = gathered[1]
    key_full = gathered[2]
    value_full = gathered[3]
    output_full = gathered[4]
    second_gain = gathered[5].astype(jnp.float32)
    router_full = gathered[6]
    residual = tokens.astype(jnp.float32)
    normed_input, first_inverse = rms_parts(residual, first_gain)
    normed_low = normed_input.astype(jnp.bfloat16)
    query_unrotated = jnp.einsum(
        "sbd,df->sbf", normed_low, query_full, preferred_element_type=jnp.float32
    ).reshape(sequences, block_rows, query_heads, head_size)
    key_unrotated = jnp.einsum(
        "sbd,df->sbf", normed_low, key_full, preferred_element_type=jnp.float32
    ).reshape(sequences, block_rows, key_heads, head_size)
    value_low = (
        jnp.einsum("sbd,df->sbf", normed_low, value_full, preferred_element_type=jnp.float32)
        .astype(jnp.bfloat16)
        .reshape(sequences, block_rows, key_heads, head_size)
    )
    query_positions = lax.axis_index("context") * block_rows + jnp.arange(
        block_rows, dtype=jnp.int32
    )
    cosine_table, sine_table = rotary_tables(query_positions.astype(jnp.float32), head_size)
    query_gain_wide = query_gain.astype(jnp.float32)
    key_gain_wide = key_gain.astype(jnp.float32)
    query_normed, query_inverse = rms_parts(query_unrotated, query_gain_wide)
    query_low = rotate(query_normed, cosine_table, sine_table).astype(jnp.bfloat16)
    key_normed, key_inverse = rms_parts(key_unrotated, key_gain_wide)
    key_low = rotate(key_normed, cosine_table, sine_table).astype(jnp.bfloat16)
    all_keys, all_values = (
        lax.all_gather(key_low, "context", axis=1, tiled=True),
        lax.all_gather(value_low, "context", axis=1, tiled=True),
    )
    grouped = query_low.reshape(sequences, block_rows, key_heads, group_size, head_size)
    key_positions = jnp.arange(length, dtype=jnp.int32)
    allowed = (key_positions[None, :] <= query_positions[:, None])[:, None, :]
    raw_scores = jnp.einsum(
        "sbkgd,slkd->skbgl", grouped, all_keys, preferred_element_type=jnp.float32
    )
    masked = jnp.where(allowed, raw_scores * score_scale, -1e30)
    highest = jnp.max(masked, axis=-1, keepdims=True)
    exponent = jnp.exp(masked - highest)
    row_total = jnp.sum(exponent, axis=-1, keepdims=True)
    probabilities = exponent / row_total
    log_total = highest + jnp.log(row_total)
    attention_mixed = jnp.einsum(
        "skbgl,slkd->sbkgd",
        probabilities.astype(jnp.bfloat16),
        all_values,
        preferred_element_type=jnp.float32,
    )
    attended_low = attention_mixed.astype(jnp.bfloat16).reshape(
        sequences, block_rows, query_heads * head_size
    )
    attention_out = lax.psum(
        jnp.einsum("sbf,fd->sbd", attended_low, output_full, preferred_element_type=jnp.float32),
        "tensor",
    )
    hidden_state = residual + attention_out
    routed_tokens, second_inverse = rms_parts(hidden_state, second_gain)
    routed_low = routed_tokens.astype(jnp.bfloat16)
    router_logits = jnp.einsum(
        "sbd,de->sbe", routed_low, router_full, preferred_element_type=jnp.float32
    )
    expert_ids = jnp.arange(expert_count, dtype=jnp.int32)
    picked_mask = routes[:, :, :, None] == expert_ids
    chosen = jnp.sum(jnp.where(picked_mask, router_logits[:, :, None, :], 0.0), axis=-1)
    top_logit = jnp.max(chosen, axis=-1, keepdims=True)
    gate_terms = jnp.exp(chosen - top_logit)
    gate_values = gate_terms / jnp.sum(gate_terms, axis=-1, keepdims=True)
    flat_routes = routes.reshape(sequences, block_rows * top_count)
    matches = (flat_routes[:, :, None] == expert_ids).astype(jnp.int32)
    slot_rank = jnp.sum((jnp.cumsum(matches, axis=1) - 1) * matches, axis=-1)
    seq_index = jnp.arange(sequences, dtype=jnp.int32)[:, None]
    destination = (flat_routes * sequences + seq_index) * capacity + slot_rank
    pair_count = sequences * block_rows * top_count
    slot_count = expert_count * sequences * capacity
    slot_pair = (
        jnp.full((slot_count,), pair_count, jnp.int32)
        .at[destination.reshape(-1)]
        .set(jnp.arange(pair_count, dtype=jnp.int32))
    )
    slot_token = jnp.where(slot_pair < pair_count, slot_pair // top_count, sequences * block_rows)
    padded_rows = jnp.concatenate(
        [
            routed_low.reshape(sequences * block_rows, model_width),
            jnp.zeros((1, model_width), jnp.bfloat16),
        ],
        axis=0,
    )
    outgoing = jnp.take(padded_rows, slot_token, axis=0).reshape(
        owners, local_experts, sequences * capacity, model_width
    )
    arrived = lax.all_to_all(outgoing, ("dp", "context"), split_axis=0, concat_axis=0, tiled=True)
    gate_hidden = jnp.einsum(
        "gesd,efd->gesf", arrived, gate_weight, preferred_element_type=jnp.float32
    )
    up_hidden = jnp.einsum("gesd,efd->gesf", arrived, up_weight, preferred_element_type=jnp.float32)
    sigmoid_gate = jax.nn.sigmoid(gate_hidden)
    activated = gate_hidden * sigmoid_gate
    inner_low = (activated * up_hidden).astype(jnp.bfloat16)
    expert_rows = jnp.einsum(
        "gesf,efd->gesd", inner_low, down_weight, preferred_element_type=jnp.float32
    ).astype(jnp.bfloat16)
    pair_rows = destination.reshape(sequences, block_rows, top_count)
    grad_out = cotangent.astype(jnp.float32)
    returned = lax.all_to_all(
        expert_rows, ("dp", "context"), split_axis=0, concat_axis=0, tiled=True
    ).reshape(slot_count, model_width)
    picked = jnp.take(returned, pair_rows, axis=0)
    experts_part = jnp.zeros((sequences, block_rows, model_width), jnp.float32)
    for pick_index in range(top_count):
        experts_part = (
            experts_part
            + gate_values[:, :, pick_index : pick_index + 1] * picked[:, :, pick_index, :]
        )
    experts_out = lax.psum(experts_part, "tensor")
    output = hidden_state + experts_out
    grad_pairs = (
        (gate_values[:, :, :, None] * grad_out[:, :, None, :])
        .astype(jnp.bfloat16)
        .reshape(pair_count, model_width)
    )
    padded_grads = jnp.concatenate([grad_pairs, jnp.zeros((1, model_width), jnp.bfloat16)], axis=0)
    grad_outgoing = jnp.take(padded_grads, slot_pair, axis=0).reshape(
        owners, local_experts, sequences * capacity, model_width
    )
    grad_arrived = lax.all_to_all(
        grad_outgoing, ("dp", "context"), split_axis=0, concat_axis=0, tiled=True
    )
    grad_inner = jnp.einsum(
        "gesd,efd->gesf", grad_arrived, down_weight, preferred_element_type=jnp.float32
    )
    down_grad = jnp.einsum(
        "gesf,gesd->efd", inner_low, grad_arrived, preferred_element_type=jnp.float32
    )
    grad_gate = (
        grad_inner * up_hidden * (sigmoid_gate + gate_hidden * sigmoid_gate * (1.0 - sigmoid_gate))
    ).astype(jnp.bfloat16)
    grad_up = (grad_inner * activated).astype(jnp.bfloat16)
    gate_grad = jnp.einsum("gesf,gesd->efd", grad_gate, arrived, preferred_element_type=jnp.float32)
    up_grad = jnp.einsum("gesf,gesd->efd", grad_up, arrived, preferred_element_type=jnp.float32)
    grad_inputs = jnp.einsum(
        "gesf,efd->gesd", grad_gate, gate_weight, preferred_element_type=jnp.float32
    )
    grad_inputs = (
        grad_inputs
        + jnp.einsum("gesf,efd->gesd", grad_up, up_weight, preferred_element_type=jnp.float32)
    ).astype(jnp.bfloat16)
    grad_returned = lax.all_to_all(
        grad_inputs, ("dp", "context"), split_axis=0, concat_axis=0, tiled=True
    ).reshape(slot_count, model_width)
    grad_picked = jnp.take(grad_returned, pair_rows, axis=0)
    grad_routed_part = jnp.zeros((sequences, block_rows, model_width), jnp.float32)
    for pick_index in range(top_count):
        grad_routed_part = grad_routed_part + grad_picked[:, :, pick_index, :]
    grad_gates_part = jnp.sum(picked.astype(jnp.float32) * grad_out[:, :, None, :], axis=-1)
    grad_routed_sum, grad_gates = lax.psum((grad_routed_part, grad_gates_part), "tensor")
    grad_chosen = gate_values * (
        grad_gates - jnp.sum(gate_values * grad_gates, axis=-1, keepdims=True)
    )
    grad_logits = jnp.sum(jnp.where(picked_mask, grad_chosen[:, :, :, None], 0.0), axis=2).astype(
        jnp.bfloat16
    )
    router_grad = jnp.einsum(
        "sbd,sbe->de", routed_low, grad_logits, preferred_element_type=jnp.float32
    )
    grad_routed = grad_routed_sum + jnp.einsum(
        "sbe,de->sbd", grad_logits, router_full, preferred_element_type=jnp.float32
    )
    grad_hidden_norm, second_gain_grad = rms_back(
        hidden_state, second_inverse, second_gain, grad_routed
    )
    grad_hidden = grad_out + grad_hidden_norm
    grad_mixed = grad_hidden.astype(jnp.bfloat16)
    output_grad = jnp.einsum(
        "sbf,sbd->fd", attended_low, grad_mixed, preferred_element_type=jnp.float32
    )
    grad_attended = (
        jnp.einsum("sbd,fd->sbf", grad_mixed, output_full, preferred_element_type=jnp.float32)
        .astype(jnp.bfloat16)
        .reshape(sequences, block_rows, key_heads, group_size, head_size)
    )
    raw_again = jnp.einsum(
        "sbkgd,slkd->skbgl", grouped, all_keys, preferred_element_type=jnp.float32
    )
    probabilities = jnp.exp(jnp.where(allowed, raw_again * score_scale, -1e30) - log_total)
    grad_probs = jnp.einsum(
        "sbkgd,slkd->skbgl", grad_attended, all_values, preferred_element_type=jnp.float32
    )
    row_delta = jnp.sum(probabilities * grad_probs, axis=-1, keepdims=True)
    grad_raw = (score_scale * probabilities * (grad_probs - row_delta)).astype(jnp.bfloat16)
    grad_query = jnp.einsum(
        "skbgl,slkd->sbkgd", grad_raw, all_keys, preferred_element_type=jnp.float32
    ).reshape(sequences, block_rows, query_heads, head_size)
    grad_keys_all = jnp.einsum(
        "skbgl,sbkgd->slkd", grad_raw, grouped, preferred_element_type=jnp.float32
    )
    grad_values_all = jnp.einsum(
        "skbgl,sbkgd->slkd",
        probabilities.astype(jnp.bfloat16),
        grad_attended,
        preferred_element_type=jnp.float32,
    )
    grad_keys, grad_values = (
        lax.psum_scatter(grad_keys_all, "context", scatter_dimension=1, tiled=True),
        lax.psum_scatter(grad_values_all, "context", scatter_dimension=1, tiled=True),
    )
    grad_query_raw, query_gain_part = rms_back(
        query_unrotated,
        query_inverse,
        query_gain_wide,
        rotate_back(grad_query, cosine_table, sine_table),
    )
    grad_key_raw, key_gain_part = rms_back(
        key_unrotated, key_inverse, key_gain_wide, rotate_back(grad_keys, cosine_table, sine_table)
    )
    grad_query_low = grad_query_raw.astype(jnp.bfloat16).reshape(
        sequences, block_rows, query_heads * head_size
    )
    grad_key_low = grad_key_raw.astype(jnp.bfloat16).reshape(
        sequences, block_rows, key_heads * head_size
    )
    grad_value_low = grad_values.astype(jnp.bfloat16).reshape(
        sequences, block_rows, key_heads * head_size
    )
    query_grad = jnp.einsum(
        "sbd,sbf->df", normed_low, grad_query_low, preferred_element_type=jnp.float32
    )
    key_grad = jnp.einsum(
        "sbd,sbf->df", normed_low, grad_key_low, preferred_element_type=jnp.float32
    )
    value_grad = jnp.einsum(
        "sbd,sbf->df", normed_low, grad_value_low, preferred_element_type=jnp.float32
    )
    grad_normed_part = jnp.einsum(
        "sbf,df->sbd", grad_query_low, query_full, preferred_element_type=jnp.float32
    )
    grad_normed_part = grad_normed_part + jnp.einsum(
        "sbf,df->sbd", grad_key_low, key_full, preferred_element_type=jnp.float32
    )
    grad_normed_part = grad_normed_part + jnp.einsum(
        "sbf,df->sbd", grad_value_low, value_full, preferred_element_type=jnp.float32
    )
    grad_normed, query_gain_sum, key_gain_sum = lax.psum(
        (grad_normed_part, query_gain_part, key_gain_part), "tensor"
    )
    grad_tokens_norm, first_gain_grad = rms_back(residual, first_inverse, first_gain, grad_normed)
    tokens_grad = grad_hidden + grad_tokens_norm
    reduced = (
        lax.psum_scatter(first_gain_grad, ("dp", "context"), scatter_dimension=0, tiled=True),
        lax.psum_scatter(query_grad, ("dp", "context"), scatter_dimension=0, tiled=True),
        lax.psum_scatter(key_grad, ("dp", "context"), scatter_dimension=0, tiled=True),
        lax.psum_scatter(value_grad, ("dp", "context"), scatter_dimension=0, tiled=True),
        lax.psum_scatter(output_grad, ("dp", "context"), scatter_dimension=1, tiled=True),
        lax.psum_scatter(second_gain_grad, ("dp", "context"), scatter_dimension=0, tiled=True),
        lax.psum_scatter(router_grad, ("dp", "context"), scatter_dimension=0, tiled=True),
        lax.psum_scatter(query_gain_sum, ("dp", "context"), scatter_dimension=0, tiled=True),
        lax.psum_scatter(key_gain_sum, ("dp", "context"), scatter_dimension=0, tiled=True),
    )
    return (
        output,
        tokens_grad,
        reduced[0],
        reduced[1],
        reduced[2],
        reduced[3],
        reduced[7],
        reduced[8],
        reduced[4],
        reduced[5],
        reduced[6],
        gate_grad,
        up_grad,
        down_grad,
    )


def solution(mesh):
    return jax.shard_map(
        per_device,
        mesh=mesh,
        in_specs=(
            P("dp", "context", None),
            P("dp", "context", None),
            P(("dp", "context")),
            P(("dp", "context"), "tensor"),
            P(("dp", "context"), "tensor"),
            P(("dp", "context"), "tensor"),
            P(),
            P(),
            P("tensor", ("dp", "context")),
            P(("dp", "context")),
            P(("dp", "context"), None),
            P(("dp", "context"), "tensor", None),
            P(("dp", "context"), "tensor", None),
            P(("dp", "context"), "tensor", None),
            P("dp", "context", None),
        ),
        out_specs=(
            P("dp", "context", None),
            P("dp", "context", None),
            P(("dp", "context")),
            P(("dp", "context"), "tensor"),
            P(("dp", "context"), "tensor"),
            P(("dp", "context"), "tensor"),
            P(("dp", "context")),
            P(("dp", "context")),
            P("tensor", ("dp", "context")),
            P(("dp", "context")),
            P(("dp", "context"), None),
            P(("dp", "context"), "tensor", None),
            P(("dp", "context"), "tensor", None),
            P(("dp", "context"), "tensor", None),
        ),
        check_vma=False,
    )
```

profile of v0, /device:TPU:1, one launch (start us, length us, event | category | flops | bytes accessed | tf_op | source)
XLA Modules:
  0.0 1493.9 jit_solution(14324280948456675710)
XLA Ops:
  14.3 66.9 %all-reduce.11 = (bf16[2048]{0:T(1024)(128)(2,1)S(1)}, bf16[2048]{0:T(1024)(128)(2,1)}) all-reduce(bf16[2048]{0:T(1024)(128)(2,1)S(1)} %dynamic-update-slice, bf16[2048]{0:T(1024)(128)(2,1)S(1)} %dynamic-update-slice.1), channel_id=1, replica_groups=mesh['dp'=4,'context'=8,'tensor'=4] {'dp','context'}, use_global_device_ids=true, to_apply=%add.2 | all-reduce | flops 4096 | bytes 16384
  82.1 27.5 %all_gather.31 = bf16[2048,128]{1,0:T(8,128)(2,1)S(1)} all-gather(bf16[64,128]{1,0:T(8,128)(2,1)} %param.21), channel_id=1, replica_groups=mesh['dp'=4,'context'=8,'tensor'=4] {'dp','context'}, dimensions={0}, use_global_device_ids=true | all-gather | bytes 540672 | tf_op jit(solution)/shard_map/all_gather | solution.py:93
  113.8 11.5 all_gather.32
  125.4 24.3 %all_gather.28 = bf16[2048,128]{1,0:T(8,128)(2,1)S(1)} all-gather(bf16[64,128]{1,0:T(8,128)(2,1)} %param.22), channel_id=1, replica_groups=mesh['dp'=4,'context'=8,'tensor'=4] {'dp','context'}, dimensions={0}, use_global_device_ids=true | all-gather | bytes 540672 | tf_op jit(solution)/shard_map/all_gather | solution.py:94
  151.3 13.0 all-gather
  166.1 2.9 fusion.130
  174.3 2.1 fusion.135
  179.6 4.8 convolution_bitcast_fusion.1
  184.4 18.0 %reduce-window.6 = s32[1,64,8,128]{3,2,1,0:T(8,128)S(1)} reduce-window(s32[1,64,8,128]{3,2,1,0:T(8,128)S(1)} %bitcast.347, s32[]{:T(128)} %constant.95.clone.1), window={size=1x1x1x128 pad=0_0x0_0x0_0x127_0}, to_apply=%region_10.11 | reduce-window | flops 8323072 | bytes 524292 | tf_op jit(solution)/shard_map/reduce-window
  203.3 4.3 scatter_custom_fusion
  207.8 18.9 %all-reduce.16.cloned.1.call-done = f32[1,128,2048]{2,1,0:T(8,128)} async-done(((f32[1,128,2048]{2,1,0:T(8,128)}), f32[1,128,2048]{2,1,0:T(8,128)}) %all-reduce.16.cloned.1.call-update) | async-done | bytes 1048592 | tf_op jit(solution)/shard_map/psum | solution.py:155
  229.6 11.0 gather_fusion
  240.6 7.5 broadcast_select_fusion.1
  248.1 9.3 all-to-all-start
  257.5 139.0 %all_gather.35 = bf16[2048,64]{1,0:T(8,128)(2,1)S(1)} all-gather(bf16[64,64]{1,0:T(8,128)(2,1)S(1)} %copy-done.54), channel_id=1, replica_groups=mesh['dp'=4,'context'=8,'tensor'=4] {'dp','context'}, dimensions={0}, use_global_device_ids=true | all-gather | bytes 270336 | tf_op jit(solution)/shard_map/all_gather | solution.py:97
  396.5 2.3 convert_bitcast_fusion.1
  399.4 1.9 fusion.1
  401.4 2.3 concatenate.61
  403.7 19.1 %gather_fusion.1 = bf16[2048,2048]{1,0:T(8,128)(2,1)} fusion(bf16[1025,2048]{1,0:T(8,128)(2,1)} %concatenate.61, s32[2048]{0:T(1024)S(1)} %get-tuple-element.58), kind=kCustom, calls=%fused_computation.3 | custom fusion | bytes 16785408 | tf_op jit(solution)/shard_map/jit(_take)/gather | solution.py:225
  422.8 7.4 broadcast_select_fusion
  430.2 7.1 all-to-all-start.2
  437.3 7.6 fusion.10
  444.9 7.2 fusion.12
  452.1 93.8 %all-to-all-done.2 = bf16[32,2,32,2048]{3,2,1,0:T(8,128)(2,1)} async-done(((bf16[32,2,32,2048]{3,2,1,0:T(8,128)(2,1)}), bf16[32,2,32,2048]{3,2,1,0:T(8,128)(2,1)}, u32[]{:S(2)}, u32[]{:S(2)}) %all-to-all-start.2) | async-done | bytes 8388640 | tf_op jit(solution)/shard_map/all_to_all | solution.py:228
  545.9 9.0 fusion.29
  555.9 5.6 convert_bitcast_fusion
  561.5 8.3 copy.202
  569.7 22.0 %all-to-all-start.1 = ((bf16[32,2,32,2048]{3,2,1,0:T(8,128)(2,1)}), bf16[32,2,32,2048]{3,2,1,0:T(8,128)(2,1)}, u32[]{:S(2)}, u32[]{:S(2)}) async-start(bf16[32,2,32,2048]{3,2,1,0:T(8,128)(2,1)} %copy.202), calls=%async_computation.1 | async-start | bytes 16777216 | tf_op jit(solution)/shard_map/all_to_all | solution.py:207
  591.7 9.4 fusion.39
  601.2 11.5 fusion
  612.6 8.3 copy.207
  621.0 79.3 %all-to-all-done.1 = bf16[32,2,32,2048]{3,2,1,0:T(8,128)(2,1)} async-done(((bf16[32,2,32,2048]{3,2,1,0:T(8,128)(2,1)}), bf16[32,2,32,2048]{3,2,1,0:T(8,128)(2,1)}, u32[]{:S(2)}, u32[]{:S(2)}) %all-to-all-start.1) | async-done | bytes 8388640 | tf_op jit(solution)/shard_map/all_to_all | solution.py:207
  700.3 20.6 %all-to-all-start.3 = ((bf16[32,2,32,2048]{3,2,1,0:T(8,128)(2,1)}), bf16[32,2,32,2048]{3,2,1,0:T(8,128)(2,1)}, u32[]{:S(2)}, u32[]{:S(2)}) async-start(bf16[32,2,32,2048]{3,2,1,0:T(8,128)(2,1)} %copy.207), calls=%async_computation.3 | async-start | bytes 16777216 | tf_op jit(solution)/shard_map/all_to_all | solution.py:250
  721.5 13.4 gather_fusion.2
  734.9 6.9 multiply_reduce_fusion
  741.8 8.6 psum.52
  750.4 79.1 %all-to-all-done.3 = bf16[32,2,32,2048]{3,2,1,0:T(8,128)(2,1)} async-done(((bf16[32,2,32,2048]{3,2,1,0:T(8,128)(2,1)}), bf16[32,2,32,2048]{3,2,1,0:T(8,128)(2,1)}, u32[]{:S(2)}, u32[]{:S(2)}) %all-to-all-start.3) | async-done | bytes 8388640 | tf_op jit(solution)/shard_map/all_to_all | solution.py:250
  829.4 13.3 gather_fusion.3
  842.7 8.8 copy_select_fusion
  853.4 4.0 fusion.57
  857.4 54.9 %all-reduce.18.cloned.1.call-done = f32[1,128,2048]{2,1,0:T(8,128)} async-done(((f32[1,128,2048]{2,1,0:T(8,128)}), f32[1,128,2048]{2,1,0:T(8,128)}) %all-reduce.18.cloned.1.call-update) | async-done | bytes 1048592 | tf_op jit(solution)/shard_map/psum | solution.py:258
  912.3 2.5 multiply_reduce_fusion.2
  917.4 2.4 fusion.15
  924.2 2.3 convolution_bitcast_fusion.3
  930.0 3.8 fusion.44
  936.2 2.5 fusion.137
  938.7 15.7 %reduce-scatter.8.cloned.1.call-done = f32[1,128,1,128]{1,3,2,0:T(8,128)} async-done(((f32[1,1024,1,128]{1,3,2,0:T(8,128)}), f32[1,128,1,128]{1,3,2,0:T(8,128)}) %reduce-scatter.8.cloned.1.call-update) | async-done | bytes 65552 | tf_op jit(solution)/shard_map/reduce_scatter | solution.py:306
  956.8 2.5 convolution_add_fusion.1
  959.3 27.8 %reduce-scatter.10.cloned.1.call-done = f32[1,128,1,128]{1,3,2,0:T(8,128)} async-done(((f32[1,1024,1,128]{1,3,2,0:T(8,128)}), f32[1,128,1,128]{1,3,2,0:T(8,128)}) %reduce-scatter.10.cloned.1.call-update) | async-done | bytes 65552 | tf_op jit(solution)/shard_map/reduce_scatter | solution.py:307
  987.2 2.7 fusion.25
  994.4 4.5 fusion.71
  999.1 4.6 fusion.126
  1005.2 7.1 fusion.22
  1012.3 7.1 fusion.19
  1019.4 31.8 %all-reduce.20.cloned.1.call-done = (f32[1,128,2048]{2,1,0:T(8,128)}, f32[1,128,2048]{2,1,0:T(8,128)}) async-done(((f32[1,128,2048]{2,1,0:T(8,128)}, f32[1,128,2048]{2,1,0:T(8,128)}), (f32[1,128,2048]{2,1,0:T(8,128)}, f32[1,128,2048]{2,1,0:T(8,128)})) %all-reduce.20.cloned.1.call-update) | async-done | bytes 2097168 | tf_op jit(solution)/shard_map/psum | solution.py:217
  1052.7 123.4 %all-reduce.8 = (f32[2048]{0:T(1024)S(1)}, f32[128]{0:T(128)S(1)}, f32[128]{0:T(128)S(1)}, f32[2048]{0:T(1024)S(1)}) all-reduce(f32[2048]{0:T(1024)S(1)} %get-tuple-element.17, f32[128]{0:T(128)S(1)} %bitcast_reduce_fusion, f32[128]{0:T(128)S(1)} %copy-done.66, ...), channel_id=5, replica_groups=mesh['dp'=4,'context'=8,'tensor'=4] {'dp','context'}, use_global_device_ids=true, to_apply=%region_29.31.clone | all-reduce | flops 4352 | bytes 34816
  1176.2 7.3 fusion.16
  1183.5 7.2 all-reduce.9
  1190.7 2.3 add.393
  1194.2 3.0 fusion.53
  1197.1 15.1 %reduce-scatter.16.cloned.1.call-done = f32[64,128]{1,0:T(8,128)} async-done(((f32[2048,128]{1,0:T(8,128)}), f32[64,128]{1,0:T(8,128)}) %reduce-scatter.16.cloned.1.call-update) | async-done | bytes 32784 | tf_op jit(solution)/shard_map/reduce_scatter | solution.py:354
  1212.3 81.6 %reduce-scatter.14.cloned.1.call-done = f32[64,128]{1,0:T(8,128)} async-done(((f32[2048,128]{1,0:T(8,128)}), f32[64,128]{1,0:T(8,128)}) %reduce-scatter.14.cloned.1.call-update) | async-done | bytes 32784 | tf_op jit(solution)/shard_map/reduce_scatter | solution.py:353
  1293.8 96.4 %reduce-scatter.18.cloned.1.call-done = f32[1024,64]{0,1:T(8,128)} async-done(((f32[1024,2048]{0,1:T(8,128)}), f32[1024,64]{0,1:T(8,128)}) %reduce-scatter.18.cloned.1.call-update) | async-done | bytes 262160 | tf_op jit(solution)/shard_map/reduce_scatter | solution.py:355
  1390.2 96.7 %reduce-scatter.12.cloned.1.call-done = f32[64,1024]{1,0:T(8,128)} async-done(((f32[2048,1024]{1,0:T(8,128)}), f32[64,1024]{1,0:T(8,128)}) %reduce-scatter.12.cloned.1.call-update) | async-done | bytes 262160 | tf_op jit(solution)/shard_map/reduce_scatter | solution.py:352
  (271 shorter events, 53.7 us)
Async XLA Ops:
  7.2 538.7 %copy-start = (bf16[2,192,2048]{2,1,0:T(8,128)(2,1)S(1)}, bf16[2,192,2048]{2,1,0:T(8,128)(2,1)}, u32[]{:S(2)}) copy-start(bf16[2,192,2048]{2,1,0:T(8,128)(2,1)} %param.30) | copy-start | bytes 4718596
  7.2 158.9 %copy-start.4 = (bf16[1,128,2048]{2,1,0:T(8,128)(2,1)S(1)}, bf16[1,128,2048]{2,1,0:T(8,128)(2,1)}, u32[]{:S(2)}) copy-start(bf16[1,128,2048]{2,1,0:T(8,128)(2,1)} %param.17) | copy-start | bytes 1572868
  7.2 158.9 %all-gather.4.cloned.1.call-start = ((), (), s32[]{:S(2)}) async-start(), calls=%async_computation.11 | async-start | bytes 4325376 | tf_op jit(solution)/shard_map/all_gather | solution.py:92
  7.9 171.6 %all-gather.6.cloned.1.call-start = ((), (), s32[]{:S(2)}) async-start(), calls=%async_computation.12 | async-start | bytes 4325376 | tf_op jit(solution)/shard_map/all_gather | solution.py:95
  8.7 217.9 %all-reduce.16.cloned.1.call-start = ((), (), s32[]{:S(2)}) async-start(), calls=%async_computation.13 | async-start | bytes 2097152 | tf_op jit(solution)/shard_map/psum | solution.py:155
  10.6 114.8 %copy-start.61 = (f32[128]{0:T(128)}, f32[128]{0:T(128)S(1)}, u32[]{:S(2)}) copy-start(f32[128]{0:T(128)S(1)} %convert_element_type.365) | copy-start | bytes 1540
  81.2 87.9 %copy-start.41 = (f32[2048]{0:T(1024)}, f32[2048]{0:T(1024)S(1)}, u32[]{:S(2)}) copy-start(f32[2048]{0:T(1024)S(1)} %convert_element_type.360) | copy-start | bytes 24580
  82.1 83.0 %copy-start.56 = (f32[128]{0:T(128)}, f32[128]{0:T(128)S(1)}, u32[]{:S(2)}) copy-start(f32[128]{0:T(128)S(1)} %fusion.122) | copy-start | bytes 1540
  82.1 83.0 %copy-start.58 = (f32[64]{0:T(128)}, f32[64]{0:T(128)S(1)}, u32[]{:S(2)}) copy-start(f32[64]{0:T(128)S(1)} %multiply_exponential_fusion) | copy-start | bytes 772
  111.5 57.5 %copy-start.51 = (f32[128]{0:T(128)}, f32[128]{0:T(128)S(1)}, u32[]{:S(2)}) copy-start(f32[128]{0:T(128)S(1)} %get-tuple-element.75) | copy-start | bytes 1540
  113.5 11.9 copy-start.63
  125.4 48.9 %copy-start.24 = (bf16[1,1024,1,128]{1,3,2,0:T(8,128)(2,1)}, bf16[1,1024,1,128]{1,3,2,0:T(8,128)(2,1)S(1)}, u32[]{:S(2)}) copy-start(bf16[1,1024,1,128]{1,3,2,0:T(8,128)(2,1)S(1)} %all_gather.32) | copy-start | bytes 786436
  149.7 19.4 %copy-start.29 = (bf16[2048,128]{1,0:T(8,128)(2,1)}, bf16[2048,128]{1,0:T(8,128)(2,1)S(1)}, u32[]{:S(2)}) copy-start(bf16[2048,128]{1,0:T(8,128)(2,1)S(1)} %all_gather.28) | copy-start | bytes 1572868
  164.3 13.3 copy-start.35
  166.0 8.2 copy-start.45
  170.0 6.4 copy-start.11
  179.6 23.1 %copy-start.65 = (bf16[2048]{0:T(1024)(128)(2,1)S(1)}, bf16[2048]{0:T(1024)(128)(2,1)}, u32[]{:S(2)}) copy-start(bf16[2048]{0:T(1024)(128)(2,1)} %get-tuple-element.30) | copy-start | bytes 12292
  248.1 9.4 copy-start.54
  248.1 150.7 %copy-start.14 = (bf16[128,2048]{1,0:T(8,128)(2,1)S(1)}, bf16[128,2048]{1,0:T(8,128)(2,1)}, u32[]{:S(2)}) copy-start(bf16[128,2048]{1,0:T(8,128)(2,1)} %copy-done.13) | copy-start | bytes 1572868
  248.1 151.0 %copy-start.49 = (s32[1,128,8]{1,2,0:T(8,128)S(1)}, s32[1,128,8]{1,2,0:T(8,128)}, u32[]{:S(2)}) copy-start(s32[1,128,8]{1,2,0:T(8,128)} %param.18) | copy-start | bytes 12292
  248.1 182.1 %all-to-all-start = ((bf16[32,2,32,2048]{3,2,1,0:T(8,128)(2,1)}), bf16[32,2,32,2048]{3,2,1,0:T(8,128)(2,1)}, u32[]{:S(2)}, u32[]{:S(2)}) async-start(bf16[32,2,32,2048]{3,2,1,0:T(8,128)(2,1)} %broadcast_select_fusion.1), calls=%async_computation | async-start | bytes 16777216 | tf_op jit(solution)/shard_map/all_to_all | solution.py:194
  430.2 115.6 %all-to-all-start.2 = ((bf16[32,2,32,2048]{3,2,1,0:T(8,128)(2,1)}), bf16[32,2,32,2048]{3,2,1,0:T(8,128)(2,1)}, u32[]{:S(2)}, u32[]{:S(2)}) async-start(bf16[32,2,32,2048]{3,2,1,0:T(8,128)(2,1)} %broadcast_select_fusion), calls=%async_computation.2 | async-start | bytes 16777216 | tf_op jit(solution)/shard_map/all_to_all | solution.py:228
  437.3 7.6 copy-start.30
  569.7 22.0 %copy-start.31 = (bf16[2,192,2048]{2,1,0:T(8,128)(2,1)S(1)}, bf16[2,192,2048]{2,1,0:T(8,128)(2,1)}, u32[]{:S(2)}) copy-start(bf16[2,192,2048]{2,1,0:T(8,128)(2,1)} %param.28) | copy-start | bytes 4718596
  569.7 130.5 %all-to-all-start.1 = ((bf16[32,2,32,2048]{3,2,1,0:T(8,128)(2,1)}), bf16[32,2,32,2048]{3,2,1,0:T(8,128)(2,1)}, u32[]{:S(2)}, u32[]{:S(2)}) async-start(bf16[32,2,32,2048]{3,2,1,0:T(8,128)(2,1)} %copy.202), calls=%async_computation.1 | async-start | bytes 16777216 | tf_op jit(solution)/shard_map/all_to_all | solution.py:207
  591.7 9.5 copy-start.32
  591.7 9.5 copy-start.39
  621.0 100.3 %copy-start.60 = (f32[128]{0:T(128)S(1)}, f32[128]{0:T(128)}, u32[]{:S(2)}) copy-start(f32[128]{0:T(128)} %convert_element_type.363) | copy-start | bytes 1540
  621.0 100.4 %copy-start.55 = (f32[128,8]{0,1:T(8,128)S(1)}, f32[128,8]{0,1:T(8,128)}, u32[]{:S(2)}) copy-start(f32[128,8]{0,1:T(8,128)} %get-tuple-element.60) | copy-start | bytes 12292
  700.3 129.2 %all-to-all-start.3 = ((bf16[32,2,32,2048]{3,2,1,0:T(8,128)(2,1)}), bf16[32,2,32,2048]{3,2,1,0:T(8,128)(2,1)}, u32[]{:S(2)}, u32[]{:S(2)}) async-start(bf16[32,2,32,2048]{3,2,1,0:T(8,128)(2,1)} %copy.207), calls=%async_computation.3 | async-start | bytes 16777216 | tf_op jit(solution)/shard_map/all_to_all | solution.py:250
  720.9 191.4 %all-reduce.18.cloned.1.call-start = ((), (), s32[]{:S(2)}) async-start(), calls=%async_computation.14 | async-start | bytes 2097152 | tf_op jit(solution)/shard_map/psum | solution.py:258
  721.5 13.4 copy-start.10
  853.2 59.1 %copy-start.17 = (bf16[2048,64]{1,0:T(8,128)(2,1)S(1)}, bf16[2048,64]{1,0:T(8,128)(2,1)}, u32[]{:S(2)}) copy-start(bf16[2048,64]{1,0:T(8,128)(2,1)} %copy-done.16) | copy-start | bytes 786436
  853.2 101.2 %reduce-scatter.8.cloned.1.call-start = ((), (), s32[]{:S(2)}) async-start(), calls=%async_computation.15 | async-start | bytes 589824 | tf_op jit(solution)/shard_map/reduce_scatter | solution.py:306
  853.3 61.5 %copy-start.26 = (bf16[1,128,2048]{2,1,0:T(8,128)(2,1)S(1)}, bf16[1,128,2048]{2,1,0:T(8,128)(2,1)}, u32[]{:S(2)}) copy-start(bf16[1,128,2048]{2,1,0:T(8,128)(2,1)} %param.31) | copy-start | bytes 1572868
  853.3 61.5 %copy-start.68 = (f32[128]{0:T(128)S(1)}, f32[128]{0:T(128)}, u32[]{:S(2)}) copy-start(f32[128]{0:T(128)} %get-tuple-element.78) | copy-start | bytes 1540
  915.2 79.1 %copy-start.7 = (f32[1,128,2048]{2,1,0:T(8,128)}, f32[1,128,2048]{2,1,0:T(8,128)S(1)}, u32[]{:S(2)}) copy-start(f32[1,128,2048]{2,1,0:T(8,128)S(1)} %convert_add_fusion.1) | copy-start | bytes 3145732
  922.3 5.0 copy-start.46
  922.3 5.0 copy-start.47
  922.3 5.3 copy-start.12
  923.7 63.4 %reduce-scatter.10.cloned.1.call-start = ((), (), s32[]{:S(2)}) async-start(), calls=%async_computation.16 | async-start | bytes 589824 | tf_op jit(solution)/shard_map/reduce_scatter | solution.py:307
  927.6 7.0 copy-start.19
  933.9 117.2 %all-reduce.20.cloned.1.call-start = ((), (), s32[]{:S(2)}) async-start(), calls=%async_computation.22 | async-start | bytes 4194304 | tf_op jit(solution)/shard_map/psum | solution.py:217
  934.6 19.8 %copy-start.57 = (f32[128]{0:T(128)S(1)}, f32[128]{0:T(128)}, u32[]{:S(2)}) copy-start(f32[128]{0:T(128)} %copy-done.56) | copy-start | bytes 1540
  934.6 19.8 %copy-start.59 = (f32[64]{0:T(128)S(1)}, f32[64]{0:T(128)}, u32[]{:S(2)}) copy-start(f32[64]{0:T(128)} %copy-done.58) | copy-start | bytes 772
  934.6 20.8 %copy-start.44 = (f32[128,128]{0,1:T(8,128)S(1)}, f32[128,128]{0,1:T(8,128)}, u32[]{:S(2)}) copy-start(f32[128,128]{0,1:T(8,128)} %copy-done.43) | copy-start | bytes 196612
  934.6 20.8 %copy-start.62 = (f32[128]{0:T(128)S(1)}, f32[128]{0:T(128)}, u32[]{:S(2)}) copy-start(f32[128]{0:T(128)} %copy-done.61) | copy-start | bytes 1540
  934.6 20.8 %copy-start.64 = (f32[128]{0:T(128)S(1)}, f32[128]{0:T(128)}, u32[]{:S(2)}) copy-start(f32[128]{0:T(128)} %copy-done.63) | copy-start | bytes 1540
  935.8 21.0 %copy-start.28 = (bf16[2048,128]{1,0:T(8,128)(2,1)S(1)}, bf16[2048,128]{1,0:T(8,128)(2,1)}, u32[]{:S(2)}) copy-start(bf16[2048,128]{1,0:T(8,128)(2,1)} %copy-done.27) | copy-start | bytes 1572868
  938.7 51.3 %copy-start.15 = (bf16[128,2048]{1,0:T(8,128)(2,1)S(1)}, bf16[128,2048]{1,0:T(8,128)(2,1)}, u32[]{:S(2)}) copy-start(bf16[128,2048]{1,0:T(8,128)(2,1)} %copy-done.13) | copy-start | bytes 1572868
  959.3 32.0 %copy-start.5 = (bf16[1,128,2048]{2,1,0:T(8,128)(2,1)S(1)}, bf16[1,128,2048]{2,1,0:T(8,128)(2,1)}, u32[]{:S(2)}) copy-start(bf16[1,128,2048]{2,1,0:T(8,128)(2,1)} %param.17) | copy-start | bytes 1572868
  959.3 32.0 %copy-start.42 = (f32[2048]{0:T(1024)S(1)}, f32[2048]{0:T(1024)}, u32[]{:S(2)}) copy-start(f32[2048]{0:T(1024)} %copy-done.41) | copy-start | bytes 24580
  959.3 32.0 %copy-start.52 = (f32[128]{0:T(128)S(1)}, f32[128]{0:T(128)}, u32[]{:S(2)}) copy-start(f32[128]{0:T(128)} %copy-done.51) | copy-start | bytes 1540
  989.9 207.2 %reduce-scatter.20.cloned.1.call-start = ((), (), s32[]{:S(2)}) async-start(), calls=%async_computation.21 | async-start | bytes 1081344 | tf_op jit(solution)/shard_map/reduce_scatter | solution.py:357
  991.3 221.0 %reduce-scatter.16.cloned.1.call-start = ((), (), s32[]{:S(2)}) async-start(), calls=%async_computation.19 | async-start | bytes 1081344 | tf_op jit(solution)/shard_map/reduce_scatter | solution.py:354
  992.8 301.0 %reduce-scatter.14.cloned.1.call-start = ((), (), s32[]{:S(2)}) async-start(), calls=%async_computation.18 | async-start | bytes 1081344 | tf_op jit(solution)/shard_map/reduce_scatter | solution.py:353
  994.3 395.9 %reduce-scatter.18.cloned.1.call-start = ((), (), s32[]{:S(2)}) async-start(), calls=%async_computation.20 | async-start | bytes 8650752 | tf_op jit(solution)/shard_map/reduce_scatter | solution.py:355
  998.9 487.9 %reduce-scatter.12.cloned.1.call-start = ((), (), s32[]{:S(2)}) async-start(), calls=%async_computation.17 | async-start | bytes 8650752 | tf_op jit(solution)/shard_map/reduce_scatter | solution.py:352
  1005.2 7.1 copy-start.40
  1012.3 7.1 copy-start.53
  1012.3 40.4 %copy-start.50 = (f32[2048]{0:T(1024)S(1)}, f32[2048]{0:T(1024)}, u32[]{:S(2)}) copy-start(f32[2048]{0:T(1024)} %get-tuple-element.15) | copy-start | bytes 24580
  1012.3 40.4 %copy-start.66 = (f32[128]{0:T(128)S(1)}, f32[128]{0:T(128)}, u32[]{:S(2)}) copy-start(f32[128]{0:T(128)} %get-tuple-element.19) | copy-start | bytes 1540
  1176.2 18.0 %copy-start.67 = (f32[128]{0:T(128)S(1)}, f32[128]{0:T(128)}, u32[]{:S(2)}) copy-start(f32[128]{0:T(128)} %get-tuple-element.74) | copy-start | bytes 1540
  1176.2 310.7 %copy-start.1 = (bf16[2,192,2048]{2,1,0:T(8,128)(2,1)S(1)}, bf16[2,192,2048]{2,1,0:T(8,128)(2,1)}, u32[]{:S(2)}) copy-start(bf16[2,192,2048]{2,1,0:T(8,128)(2,1)} %param.30) | copy-start | bytes 4718596
  (21 other events, 51.1 us)
Sparse Core Ops, SparseCore 0:
  10.3 50.2 all-gather.3
  62.8 46.2 all-gather.5
  184.5 42.0 all-reduce.15
  853.3 58.9 all-reduce.17
  923.9 30.4 reduce-scatter.7
  957.3 29.8 reduce-scatter.9
  990.7 60.3 all-reduce.19
  1055.6 75.8 reduce-scatter.19
  1135.6 76.6 reduce-scatter.15
  1216.6 77.2 reduce-scatter.13
  1298.1 92.0 reduce-scatter.17
  1394.8 92.0 reduce-scatter.11
where the time goes:
time: 1500 us; the launch traced here: 1490 us
  waiting for transfers between devices  693 us (46%)
  blocking collectives  421 us (28%)
  matrix products  120 us (8%)
  local copies, waits for them, and re-layouts  97.3 us (6%)
  other arithmetic  85 us (6%)
  starting transfers between devices  60 us (4%)
  between operations  17.5 us (1%)
    unnamed x2, blocking collectives  190 us
    all_gather x1, blocking collectives, per_device(): lax.all_gather(router_matrix, ('dp', 'context'), axis=0, tiled=True)  139 us
    reduce_scatter x1, waiting for transfers between devices, per_device(): lax.psum_scatter(query_grad, ('dp', 'context'), scatter_dimension=0, tile...  96.7 us
    reduce_scatter x1, waiting for transfers between devices, per_device(): lax.psum_scatter(output_grad, ('dp', 'context'), scatter_dimension=1, til...  96.4 us
    all_to_all x1, waiting for transfers between devices, per_device(): lax.all_to_all(grad_outgoing, ('dp', 'context'), split_axis=0, concat_axi...  93.8 us
    reduce_scatter x1, waiting for transfers between devices, per_device(): lax.psum_scatter(key_grad, ('dp', 'context'), scatter_dimension=0, tiled=...  81.6 us
    all_to_all x1, waiting for transfers between devices, per_device(): lax.all_to_all(expert_rows, ('dp', 'context'), split_axis=0, concat_axis=...  79.3 us
    all_to_all x1, waiting for transfers between devices, per_device(): lax.all_to_all(grad_inputs, ('dp', 'context'), split_axis=0, concat_axis=...  79.1 us
  transfers between devices with their start and end apart: 16, of which 12 were waited for; matrix products, arithmetic and copies ran while one was open for 14% of the time, Pallas kernels for 0%

commit v1 on v0

v1 whole, which is shorter than its diff:
```python
import functools
import math

import jax
import jax.numpy as jnp
from jax import lax
from jax.experimental import pallas as pl
from jax.experimental.pallas import tpu as pltpu
from jax.sharding import PartitionSpec as P

MESH = pl.DeviceIdType.MESH
F32 = jnp.float32
BF16 = jnp.bfloat16
MIB = 1 << 20


class Links:
    def __init__(self, send_sem, recv_sem):
        self.send_sem, self.recv_sem = send_sem, recv_sem
        self.copies = []

    def send(self, source, target, device, arriving):
        index = len(self.copies)
        copy = pltpu.make_async_remote_copy(
            src_ref=source,
            dst_ref=target,
            send_sem=self.send_sem.at[index],
            recv_sem=self.recv_sem.at[index],
            device_id=device,
            device_id_type=MESH,
        )
        copy.start()
        landing = pltpu.make_async_remote_copy(
            src_ref=arriving,
            dst_ref=arriving,
            send_sem=self.send_sem.at[index],
            recv_sem=self.recv_sem.at[index],
            device_id=device,
            device_id_type=MESH,
        )
        self.copies.append(copy)
        return landing

    def finish(self):
        for copy in self.copies:
            copy.wait_send()


def greet(devices):
    barrier = pltpu.get_barrier_semaphore()
    for device in devices:
        pl.semaphore_signal(barrier, inc=1, device_id=device, device_id_type=MESH)
    pl.semaphore_wait(barrier, len(devices))


def plane_place():
    y = lax.axis_index("dp")
    position = lax.axis_index("context")
    z = position // 2
    core = position - 2 * z

    def device(step):
        return {"dp": (y + step[0]) % 4, "context": ((z + step[1]) % 4) * 2 + core}

    def slot(step, other=False):
        at = 1 - core if other else core
        return ((y + step[0]) % 4) * 8 + ((z + step[1]) % 4) * 2 + at

    sibling = {"context": 2 * z + 1 - core}
    return device, slot, sibling


def along(first, second, order):
    return (first, second) if order == 0 else (second, first)


NEAR = ((1, 0), (-1, 0), (0, 1), (0, -1))


def gather_body(count, *refs):
    mine, whole = refs[:count], refs[count : 2 * count]
    send_sem, recv_sem, own_sem = refs[2 * count :]
    device, slot, sibling = plane_place()
    greet([device(step) for step in NEAR] + [sibling])
    links = Links(send_sem, recv_sem)
    jobs = [(a, order) for a in range(count) for order in range(2)]

    def rows_of(a, order, part):
        rows = mine[a].shape[0]
        start, size = order * (rows // 2), rows // 2
        if part == 2:
            return 0, rows
        if part == 1:
            return start + size // 2, size // 2
        if part == 0:
            return start, size // 2
        return start, size

    def region(a, order, place, part, other=False):
        rows = mine[a].shape[0]
        start, size = rows_of(a, order, part)
        base = pl.multiple_of(slot(along(*place, order), other) * rows + start, 16)
        return whole[a].at[pl.ds(base, size)]

    def push(a, order, place, part, axis, sign):
        step = along(sign, 0, order) if axis == 0 else along(0, sign, order)
        source = region(a, order, place, part)
        if place == (0, 0):
            start, size = rows_of(a, order, part)
            source = mine[a].at[pl.ds(start, size)]
        came = (place[0] - sign, place[1]) if axis == 0 else (place[0], place[1] - sign)
        return links.send(
            source, region(a, order, place, part), device(step), region(a, order, came, part)
        )

    beside = []

    def share(a, order, place, part=None):
        source = mine[a] if part == 2 else region(a, order, place, part)
        beside.append(
            links.send(
                source,
                region(a, order, place, part),
                sibling,
                region(a, order, place, part, True),
            )
        )

    own = []
    for a in range(count):
        copy = pltpu.make_async_copy(mine[a], region(a, 0, (0, 0), 2), own_sem.at[a])
        copy.start()
        own.append(copy)
    got = {}
    for a, order in jobs:
        for sign in (1, -1):
            got[a, order, sign] = push(a, order, (0, 0), None, 0, sign)
    for a, order in jobs:
        for sign in (1, -1):
            got[a, order, 0, sign] = push(a, order, (0, 0), None, 1, sign)
    for a in range(count):
        share(a, 0, (0, 0), 2)
    for a, order in jobs:
        for sign in (1, -1):
            got[a, order, sign].wait_recv()
            got[a, order, "far", sign] = push(
                a, order, (-sign, 0), 0 if sign == 1 else 1, 0, sign
            )
        for sign in (1, -1):
            for way in (1, -1):
                got[a, order, -sign, way] = push(a, order, (-sign, 0), None, 1, way)
            share(a, order, (-sign, 0))
    for a, order in jobs:
        for sign in (1, -1):
            got[a, order, "far", sign].wait_recv()
        for way in (1, -1):
            got[a, order, 2, way] = push(a, order, (2, 0), None, 1, way)
        share(a, order, (2, 0))
    for i in (0, 1, -1, 2):
        for a, order in jobs:
            for way in (1, -1):
                got[a, order, i, way].wait_recv()
                got[a, order, i, "far", way] = push(
                    a, order, (i, -way), 0 if way == 1 else 1, 1, way
                )
                share(a, order, (i, -way))
    for i in (0, 1, -1, 2):
        for a, order in jobs:
            for way in (1, -1):
                got[a, order, i, "far", way].wait_recv()
            share(a, order, (i, 2))
    for copy in beside:
        copy.wait_recv()
    for copy in own:
        copy.wait()
    links.finish()


def gather_copies(count):
    return count * (2 * 20 + 1 + 2 * 15)


def plane_gather(arrays, collective_id):
    count = len(arrays)
    copies = gather_copies(count)
    return pl.pallas_call(
        functools.partial(gather_body, count),
        out_shape=[
            jax.ShapeDtypeStruct((32 * a.shape[0],) + a.shape[1:], a.dtype) for a in arrays
        ],
        in_specs=[pl.BlockSpec(memory_space=pl.ANY)] * count,
        out_specs=[pl.BlockSpec(memory_space=pl.ANY)] * count,
        scratch_shapes=[
            pltpu.SemaphoreType.DMA((copies,)),
            pltpu.SemaphoreType.DMA((copies,)),
            pltpu.SemaphoreType.DMA((count,)),
        ],
        compiler_params=pltpu.CompilerParams(
            collective_id=collective_id, has_side_effects=True, vmem_limit_bytes=16 * MIB
        ),
    )(*arrays)


def add_rows(target, sources, offset, size, chunk=16):
    def step(k, carry):
        base = pl.multiple_of(k * chunk, chunk)
        at = pl.ds(offset + base, chunk)
        total = target[at].astype(F32)
        for source, start in sources:
            total = total + source[pl.ds(start + base, chunk)].astype(F32)
        target[at] = total.astype(target.dtype)
        return carry

    lax.fori_loop(0, size // chunk, step, 0)


SLOTS = (
    (2, 2), (1, 2), (2, 1), (-1, 2), (2, -1), (0, 2), (2, 0),
    (1, 1), (1, -1), (-1, 1), (-1, -1), (0, 1), (1, 0), (0, -1), (-1, 0), (0, 0),
)


def scatter_body(rows, part_ref, out_ref, held, near, landed, send_sem, recv_sem, own_sem):
    device, slot, sibling = plane_place()
    greet([device(step) for step in NEAR] + [sibling])
    links = Links(send_sem, recv_sem)
    half, quarter = rows // 2, rows // 4
    index = {place: k for k, place in enumerate(SLOTS)}

    def base(place):
        return index[place] * rows

    loads, shares = {}, {}
    for k, place in enumerate(SLOTS):
        copy = pltpu.make_async_copy(
            part_ref.at[pl.ds(pl.multiple_of(slot(place) * rows, 16), rows)],
            held.at[pl.ds(base(place), rows)],
            own_sem.at[k],
        )
        copy.start()
        loads[place] = copy
        here = near.at[pl.ds(base(place), rows)]
        shares[place] = links.send(
            part_ref.at[pl.ds(pl.multiple_of(slot(place, True) * rows, 16), rows)],
            here,
            sibling,
            here,
        )
    merged = set()

    def ready(order, place):
        place = along(*place, order)
        if place not in merged:
            merged.add(place)
            loads[place].wait()
            shares[place].wait_recv()
            add_rows(held, [(near, base(place))], base(place), rows)
        return base(place) + order * half

    room = [0]

    def push(start, size, order, axis, sign):
        step = along(sign, 0, order) if axis == 0 else along(0, sign, order)
        at = room[0]
        room[0] += size
        here = landed.at[pl.ds(at, size)]
        return links.send(held.at[pl.ds(start, size)], here, device(step), here), at

    got = {}

    def reduce_ring(key, order, axis, places, stage):
        opposite, plus, minus, mine = places
        if stage == 0:
            start = ready(order, opposite)
            got[key, 0] = push(start, quarter, order, axis, 1)
            got[key, 1] = push(start + quarter, quarter, order, axis, -1)
        if stage == 1:
            start = ready(order, plus)
            copy, at = got[key, 0]
            copy.wait_recv()
            add_rows(held, [(landed, at)], start, quarter)
            got[key, 2] = push(start, half, order, axis, 1)
            start = ready(order, minus)
            copy, at = got[key, 1]
            copy.wait_recv()
            add_rows(held, [(landed, at)], start + quarter, quarter)
            got[key, 3] = push(start, half, order, axis, -1)
        if stage == 2:
            start = ready(order, mine)
            sources = []
            for k in (2, 3):
                copy, at = got[key, k]
                copy.wait_recv()
                sources.append((landed, at))
            if axis == 1:
                add_rows(held, sources, start, half)
            else:
                for k in range(half // 16):
                    total = held[pl.ds(start + 16 * k, 16)].astype(F32)
                    for source, at in sources:
                        total = total + source[pl.ds(at + 16 * k, 16)].astype(F32)
                    out_ref[pl.ds(order * half + 16 * k, 16)] = total

    def ring(i, order, stage):
        reduce_ring((order, i), order, 1, [(i, j) for j in (2, 1, -1, 0)], stage)

    def last(order, stage):
        reduce_ring((order, "last"), order, 0, [(i, 0) for i in (2, 1, -1, 0)], stage)

    for i in (2, 1, -1, 0):
        for order in range(2):
            ring(i, order, 0)
    for i in (2, 1, -1, 0):
        for order in range(2):
            ring(i, order, 1)
    for order in range(2):
        ring(2, order, 2)
        last(order, 0)
    for order in range(2):
        ring(1, order, 2)
        ring(-1, order, 2)
        last(order, 1)
    for order in range(2):
        ring(0, order, 2)
        last(order, 2)
    links.finish()


def plane_scatter(part, collective_id):
    rows, columns = part.shape[0] // 32, part.shape[1]
    copies = 16 + 2 * 20
    vmem = (2 * 16 + 15) * rows * columns * 2 + 2 * rows * columns * 4 + 4 * MIB
    return pl.pallas_call(
        functools.partial(scatter_body, rows),
        out_shape=jax.ShapeDtypeStruct((rows, columns), F32),
        in_specs=[pl.BlockSpec(memory_space=pl.ANY)],
        out_specs=pl.BlockSpec(memory_space=pltpu.VMEM),
        scratch_shapes=[
            pltpu.VMEM((16 * rows, columns), BF16),
            pltpu.VMEM((16 * rows, columns), BF16),
            pltpu.VMEM((15 * rows, columns), BF16),
            pltpu.SemaphoreType.DMA((copies,)),
            pltpu.SemaphoreType.DMA((copies,)),
            pltpu.SemaphoreType.DMA((16,)),
        ],
        compiler_params=pltpu.CompilerParams(
            collective_id=collective_id, has_side_effects=True, vmem_limit_bytes=vmem
        ),
    )(part)


def tensor_sum_body(count, *refs):
    parts, outs = refs[:count], refs[count : 2 * count]
    held, landed = refs[2 * count : 3 * count], refs[3 * count : 4 * count]
    send_sem, recv_sem = refs[4 * count :]
    x = lax.axis_index("tensor")

    def device(step):
        return {"tensor": (x + step) % 4}

    greet([device(1), device(-1)])
    links = Links(send_sem, recv_sem)
    got = {}

    def rows(a, step, start, size):
        quarter = parts[a].shape[0] // 4
        return pl.ds(pl.multiple_of(((x + step) % 4) * quarter + start, 16), size)

    def push(a, source, sign, at, size):
        here = landed[a].at[pl.ds(at, size)]
        return links.send(source, here, device(sign), here)

    for a in range(count):
        held[a][...] = parts[a][...].astype(BF16)
        quarter = parts[a].shape[0] // 4
        eighth = quarter // 2
        got[a, 0] = push(a, held[a].at[rows(a, 2, 0, eighth)], 1, 0, eighth)
        got[a, 1] = push(a, held[a].at[rows(a, 2, eighth, eighth)], -1, eighth, eighth)
    for a in range(count):
        quarter = parts[a].shape[0] // 4
        eighth = quarter // 2
        for k, sign in enumerate((1, -1)):
            got[a, k].wait_recv()
            at = rows(a, sign, k * eighth, eighth)
            total = parts[a][at].astype(F32) + landed[a][k * eighth : (k + 1) * eighth].astype(F32)
            held[a][at] = total.astype(BF16)
            got[a, 2 + k] = push(
                a, held[a].at[rows(a, sign, 0, quarter)], sign, (k + 1) * quarter, quarter
            )
    for a in range(count):
        quarter = parts[a].shape[0] // 4
        got[a, 2].wait_recv()
        got[a, 3].wait_recv()
        mine = rows(a, 0, 0, quarter)
        total = parts[a][mine].astype(F32)
        total = total + landed[a][quarter : 2 * quarter].astype(F32)
        total = total + landed[a][2 * quarter : 3 * quarter].astype(F32)
        outs[a][mine] = total.astype(BF16)
        for k, sign in enumerate((1, -1)):
            got[a, 4 + k] = links.send(
                outs[a].at[mine], outs[a].at[mine], device(sign),
                outs[a].at[rows(a, -sign, 0, quarter)],
            )
    for a in range(count):
        quarter = parts[a].shape[0] // 4
        eighth = quarter // 2
        for k, sign in enumerate((1, -1)):
            got[a, 4 + k].wait_recv()
            at = rows(a, -sign, k * eighth, eighth)
            got[a, 6 + k] = links.send(
                outs[a].at[at], outs[a].at[at], device(sign),
                outs[a].at[rows(a, 2, k * eighth, eighth)],
            )
    for a in range(count):
        got[a, 6].wait_recv()
        got[a, 7].wait_recv()
    links.finish()


def tensor_sum(arrays, collective_id):
    count = len(arrays)
    spec = pl.BlockSpec(memory_space=pltpu.VMEM)
    return pl.pallas_call(
        functools.partial(tensor_sum_body, count),
        out_shape=[jax.ShapeDtypeStruct(a.shape, BF16) for a in arrays],
        in_specs=[spec] * count,
        out_specs=[spec] * count,
        scratch_shapes=[pltpu.VMEM(a.shape, BF16) for a in arrays]
        + [pltpu.VMEM((a.shape[0] * 3 // 4, a.shape[1]), BF16) for a in arrays]
        + [pltpu.SemaphoreType.DMA((8 * count,)), pltpu.SemaphoreType.DMA((8 * count,))],
        compiler_params=pltpu.CompilerParams(
            collective_id=collective_id, has_side_effects=True, vmem_limit_bytes=32 * MIB
        ),
    )(*arrays)


def context_place():
    position = lax.axis_index("context")

    def device(step):
        return {"context": (position + step) % 8}

    return position, device


def context_gather_body(mine, whole, send_sem, recv_sem, own_sem):
    position, device = context_place()
    rows = mine.shape[0]
    greet([device(step) for step in range(1, 8)])
    links = Links(send_sem, recv_sem)

    def region(step):
        return whole.at[pl.ds(pl.multiple_of(((position + step) % 8) * rows, 16), rows)]

    own = pltpu.make_async_copy(mine, region(0), own_sem)
    own.start()
    got = [links.send(mine, region(0), device(step), region(-step)) for step in range(1, 8)]
    for copy in got:
        copy.wait_recv()
    own.wait()
    links.finish()


def context_gather(array, collective_id):
    spec = pl.BlockSpec(memory_space=pltpu.VMEM)
    return pl.pallas_call(
        context_gather_body,
        out_shape=jax.ShapeDtypeStruct((8 * array.shape[0],) + array.shape[1:], array.dtype),
        in_specs=[spec],
        out_specs=spec,
        scratch_shapes=[
            pltpu.SemaphoreType.DMA((7,)),
            pltpu.SemaphoreType.DMA((7,)),
            pltpu.SemaphoreType.DMA,
        ],
        compiler_params=pltpu.CompilerParams(collective_id=collective_id, has_side_effects=True),
    )(array)


def context_scatter_body(part, out, landed, send_sem, recv_sem):
    position, device = context_place()
    rows = out.shape[0]
    greet([device(step) for step in range(1, 8)])
    links = Links(send_sem, recv_sem)

    def region(step):
        return pl.ds(pl.multiple_of(((position + step) % 8) * rows, 16), rows)

    got = []
    for step in range(1, 8):
        here = landed.at[pl.ds((step - 1) * rows, rows)]
        got.append(links.send(part.at[region(step)], here, device(step), here))
    total = part[region(0)].astype(F32)
    for k, copy in enumerate(got):
        copy.wait_recv()
        total = total + landed[k * rows : (k + 1) * rows].astype(F32)
    out[...] = total
    links.finish()


def context_scatter(part, collective_id):
    rows, columns = part.shape[0] // 8, part.shape[1]
    spec = pl.BlockSpec(memory_space=pltpu.VMEM)
    return pl.pallas_call(
        context_scatter_body,
        out_shape=jax.ShapeDtypeStruct((rows, columns), F32),
        in_specs=[spec],
        out_specs=spec,
        scratch_shapes=[
            pltpu.VMEM((7 * rows, columns), part.dtype),
            pltpu.SemaphoreType.DMA((7,)),
            pltpu.SemaphoreType.DMA((7,)),
        ],
        compiler_params=pltpu.CompilerParams(
            collective_id=collective_id, has_side_effects=True, vmem_limit_bytes=24 * MIB
        ),
    )(part)


def dot(a, b, contract):
    return lax.dot_general(a, b, (contract, ((), ())), preferred_element_type=F32)


PAIR = 256
STEP = 512
CAPACITY = 32


def experts_body(
    steps, width, x_ref, c_ref, row_ref, column_ref, gate_ref, lane_ref, wg_ref, wu_ref, wd_ref,
    out_ref, back_ref, gg_ref, gu_ref, gd_ref, rows, pairs, inner, slope_g, slope_u,
):
    step = pl.program_id(0)
    local = wg_ref.shape[0]
    per_pair = 2 * CAPACITY
    pair_count = STEP // PAIR
    per_step = pair_count * per_pair

    @pl.when(step < steps)
    def _():
        base = pl.multiple_of(step * per_step, per_step)
        weights = [[None] * pair_count for _ in range(local)]
        for p in range(pair_count):
            tokens = pl.ds(p * PAIR, PAIR)
            picks = []
            slots = lax.broadcasted_iota(jnp.int32, (per_pair, PAIR), 0)
            for e in range(local):
                match = slots == row_ref[e : e + 1, tokens]
                weights[e][p] = jnp.sum(
                    jnp.where(match, gate_ref[e : e + 1, tokens], 0.0), axis=1, keepdims=True
                )
                picks.append(jnp.where(match, 1.0, 0.0).astype(BF16))
            pick = jnp.concatenate(picks, axis=0)
            taken = dot(pick, x_ref[tokens, :width], ((1,), (0,))).astype(BF16)
            given = dot(pick, c_ref[tokens, :width], ((1,), (0,)))
            for e in range(local):
                at = pl.ds(base + p * per_pair, per_pair)
                mine = slice(e * per_pair, (e + 1) * per_pair)
                rows[e, at] = taken[mine]
                pairs[e, at] = (weights[e][p] * given[mine]).astype(BF16)
        sent, returned = [], []
        for e in range(local):
            at = pl.ds(base, per_step)
            weight = jnp.concatenate(weights[e], axis=0)
            taken, given = rows[e, at], pairs[e, at]
            gate = dot(taken, wg_ref[e], ((1,), (1,)))
            up = dot(taken, wu_ref[e], ((1,), (1,)))
            grad_inner = dot(given, wd_ref[e], ((1,), (1,)))
            sigmoid = jax.nn.sigmoid(gate)
            active = gate * sigmoid
            hidden = (active * up).astype(BF16)
            inner[e, at] = hidden
            sent.append((dot(hidden, wd_ref[e], ((1,), (0,))) * weight).astype(BF16))
            share = jnp.sum(hidden.astype(F32) * grad_inner, axis=1, keepdims=True)
            grad_gate = (grad_inner * up * sigmoid * (1.0 + gate * (1.0 - sigmoid))).astype(BF16)
            grad_up = (grad_inner * active).astype(BF16)
            slope_g[e, at] = grad_gate
            slope_u[e, at] = grad_up
            grad = dot(grad_gate, wg_ref[e], ((1,), (0,)))
            grad = grad + dot(grad_up, wu_ref[e], ((1,), (0,)))
            high = share.astype(BF16).astype(F32)
            lanes = high * lane_ref[2 * e : 2 * e + 1] + (share - high) * lane_ref[2 * e + 1 : 2 * e + 2]
            returned.append((grad.astype(BF16), lanes.astype(BF16)))
        lane_slots = lax.broadcasted_iota(jnp.int32, (PAIR, per_pair), 1)
        for p in range(pair_count):
            tokens = pl.ds(p * PAIR, PAIR)
            mine = slice(p * per_pair, (p + 1) * per_pair)
            places = [
                jnp.where(lane_slots == column_ref[tokens, e : e + 1], 1.0, 0.0).astype(BF16)
                for e in range(local)
            ]
            place = jnp.concatenate(places, axis=1)
            out_rows = jnp.concatenate([s[mine] for s in sent], axis=0)
            out_ref[tokens] = dot(place, out_rows, ((1,), (0,))).astype(BF16)
            back_rows = jnp.concatenate([r[0][mine] for r in returned], axis=0)
            back_ref[tokens, :width] = dot(place, back_rows, ((1,), (0,))).astype(BF16)
            lane_rows = jnp.concatenate([r[1][mine] for r in returned], axis=0)
            back_ref[tokens, width:] = dot(place, lane_rows, ((1,), (0,))).astype(BF16)

    @pl.when(step >= steps)
    def _():
        e = step - steps
        gd_ref[0] = dot(inner[e], pairs[e], ((0,), (0,)))
        gg_ref[0] = dot(slope_g[e], rows[e], ((0,), (0,)))
        gu_ref[0] = dot(slope_u[e], rows[e], ((0,), (0,)))


def experts(x, c, row, column, gate, lanes, wg, wu, wd):
    count, local, units, width = x.shape[0], wg.shape[0], wg.shape[1], wg.shape[2]
    steps = count // STEP
    slots = count // 128 * CAPACITY

    def tokens(s):
        return (jnp.minimum(s, steps - 1), 0)

    def lanes_of(s):
        return (0, jnp.minimum(s, steps - 1))

    def fixed(*shape):
        return pl.BlockSpec(
            shape, lambda s: (0,) * len(shape), pipeline_mode=pl.Buffered(buffer_count=1)
        )

    def weight_out(s):
        return (jnp.maximum(s - steps, 0), 0, 0)

    flops = 2 * (9 * local * slots * units * width + 4 * local * slots * PAIR * width)
    return pl.pallas_call(
        functools.partial(experts_body, steps, width),
        grid=(steps + local,),
        out_shape=[
            jax.ShapeDtypeStruct((count, width), BF16),
            jax.ShapeDtypeStruct((count, width + 128), BF16),
        ]
        + [jax.ShapeDtypeStruct((local, units, width), F32)] * 3,
        in_specs=[
            pl.BlockSpec((STEP, x.shape[1]), tokens),
            pl.BlockSpec((STEP, c.shape[1]), tokens),
            pl.BlockSpec((local, STEP), lanes_of),
            pl.BlockSpec((STEP, local), tokens),
            pl.BlockSpec((local, STEP), lanes_of),
            fixed(2 * local, 128),
            fixed(local, units, width),
            fixed(local, units, width),
            fixed(local, units, width),
        ],
        out_specs=[
            pl.BlockSpec((STEP, width), tokens),
            pl.BlockSpec((STEP, width + 128), tokens),
        ]
        + [pl.BlockSpec((1, units, width), weight_out)] * 3,
        scratch_shapes=[
            pltpu.VMEM((local, slots, width), BF16),
            pltpu.VMEM((local, slots, width), BF16),
            pltpu.VMEM((local, slots, units), BF16),
            pltpu.VMEM((local, slots, units), BF16),
            pltpu.VMEM((local, slots, units), BF16),
        ],
        compiler_params=pltpu.CompilerParams(vmem_limit_bytes=63 * MIB),
        cost_estimate=pl.CostEstimate(
            flops=flops, bytes_accessed=80 * MIB, transcendentals=2 * slots * units
        ),
    )(x, c, row, column, gate, lanes, wg, wu, wd)


EPSILON = 1e-06
THETA = 1000000.0
PLANE = ("dp", "context")


def rms_parts(values, gain_vector):
    inverse = lax.rsqrt(jnp.mean(values * values, axis=-1, keepdims=True) + EPSILON)
    return (values * inverse * gain_vector, inverse)


def rms_back(values, inverse, gain_vector, grad_out):
    scaled = grad_out * gain_vector
    inner_mean = jnp.mean(scaled * values, axis=-1, keepdims=True)
    grad_in = inverse * scaled - values * (inverse * inverse * inverse) * inner_mean
    leading = tuple(range(values.ndim - 1))
    grad_gain = jnp.sum(grad_out * values * inverse, axis=leading)
    return (grad_in, grad_gain)


def rotary_tables(positions, head_size):
    half_size = head_size // 2
    frequency = jnp.exp(jnp.arange(half_size, dtype=F32) * (-2.0 * math.log(THETA) / head_size))
    angles = positions[:, None] * frequency[None, :]
    return (jnp.cos(angles)[:, None, :], jnp.sin(angles)[:, None, :])


def rotate(values, cosine_table, sine_table):
    half_size = values.shape[-1] // 2
    first_half = values[..., :half_size]
    second_half = values[..., half_size:]
    return jnp.concatenate(
        [
            first_half * cosine_table - second_half * sine_table,
            second_half * cosine_table + first_half * sine_table,
        ],
        axis=-1,
    )


def rotate_back(grad_out, cosine_table, sine_table):
    return rotate(grad_out, cosine_table, -sine_table)


def matmul(a, b, contract=((1,), (0,))):
    return lax.dot_general(a, b, (contract, ((), ())), preferred_element_type=F32)


def split_high(values):
    high = values.astype(BF16)
    return high, (values - high.astype(F32)).astype(BF16)


def per_device(
    tokens, routes, attention_gain, query_matrix, key_matrix, value_matrix, query_gain, key_gain,
    output_matrix, experts_gain, router_matrix, gate_weight, up_weight, down_weight, cotangent,
):
    tokens, routes, cotangent = tokens[0], routes[0], cotangent[0]
    rows, width = tokens.shape
    expert_count = router_matrix.shape[1]
    local = gate_weight.shape[0]
    head = query_gain.shape[0]
    query_columns, key_columns = query_matrix.shape[1], key_matrix.shape[1]
    heads = query_columns // head
    owners = 32
    shard = width // owners
    length = rows * 8
    scale = head ** (-0.5)
    qkv_columns = query_columns + 2 * key_columns

    packed = jnp.concatenate(
        [
            query_matrix,
            key_matrix,
            value_matrix,
            output_matrix.T,
            router_matrix,
            attention_gain[:, None],
            experts_gain[:, None],
            jnp.zeros((shard, 128 - expert_count - 2), BF16),
        ],
        axis=1,
    )
    (weights,) = plane_gather([packed], 0)
    qkv_matrix = weights[:, :qkv_columns]
    output_turned = weights[:, qkv_columns : qkv_columns + query_columns]
    rest = weights[:, qkv_columns + query_columns :]
    router = rest[:, :expert_count]
    first_gain = rest[:, expert_count].astype(F32)
    second_gain = rest[:, expert_count + 1].astype(F32)

    expert_ids = jnp.arange(expert_count, dtype=jnp.int32)
    mask = jnp.any(routes[:, :, None] == expert_ids, axis=1)
    sent_mask = jnp.pad(mask.astype(BF16), ((0, 0), (0, 128 - expert_count)))
    (all_grads,) = plane_gather([jnp.concatenate([cotangent, sent_mask], axis=1)], 1)

    residual = tokens.astype(F32)
    normed_input, first_inverse = rms_parts(residual, first_gain)
    normed_low = normed_input.astype(BF16)
    qkv = matmul(normed_low, qkv_matrix)
    query_unrotated = qkv[:, :query_columns].reshape(rows, heads, head)
    key_unrotated = qkv[:, query_columns : query_columns + key_columns].reshape(rows, 1, head)
    value_low = qkv[:, query_columns + key_columns :].astype(BF16)
    positions = lax.axis_index("context") * rows + jnp.arange(rows, dtype=jnp.int32)
    cosine_table, sine_table = rotary_tables(positions.astype(F32), head)
    query_gain_wide, key_gain_wide = query_gain.astype(F32), key_gain.astype(F32)
    query_normed, query_inverse = rms_parts(query_unrotated, query_gain_wide)
    query_low = rotate(query_normed, cosine_table, sine_table).astype(BF16)
    key_normed, key_inverse = rms_parts(key_unrotated, key_gain_wide)
    key_low = rotate(key_normed, cosine_table, sine_table).astype(BF16).reshape(rows, head)
    both = context_gather(jnp.concatenate([key_low, value_low], axis=1), 2)
    all_keys, all_values = both[:, :head], both[:, head:]
    allowed = (jnp.arange(length, dtype=jnp.int32)[None, :] <= positions[:, None])[:, None, :]
    raw_scores = jnp.einsum("bgd,ld->bgl", query_low, all_keys, preferred_element_type=F32)
    masked = jnp.where(allowed, raw_scores * scale, -1e30)
    highest = jnp.max(masked, axis=-1, keepdims=True)
    exponent = jnp.exp(masked - highest)
    row_total = jnp.sum(exponent, axis=-1, keepdims=True)
    probabilities = exponent / row_total
    log_total = highest + jnp.log(row_total)
    attended = jnp.einsum(
        "bgl,ld->bgd", probabilities.astype(BF16), all_values, preferred_element_type=F32
    )
    attended_low = attended.astype(BF16).reshape(rows, query_columns)
    attention_part = matmul(attended_low, output_turned, ((1,), (1,)))
    (attention_out,) = tensor_sum([attention_part], 3)
    hidden_state = residual + attention_out.astype(F32)
    routed_tokens, second_inverse = rms_parts(hidden_state, second_gain)
    routed_low = routed_tokens.astype(BF16)
    logits = matmul(routed_low, router)
    chosen = jnp.where(mask, logits, -1e30)
    gate_terms = jnp.where(mask, jnp.exp(chosen - jnp.max(chosen, axis=-1, keepdims=True)), 0.0)
    gates = gate_terms / jnp.sum(gate_terms, axis=-1, keepdims=True)
    gates_high, gates_low = split_high(gates)
    (all_rows,) = plane_gather([jnp.concatenate([routed_low, gates_high, gates_low], axis=1)], 4)

    first_expert = (lax.axis_index("dp") * 8 + lax.axis_index("context")) * local
    here = lax.dynamic_slice(all_grads, (0, width + first_expert), (all_grads.shape[0], local))
    blocks = here.reshape(owners, rows, local)
    before = jnp.tril(jnp.ones((rows, rows), BF16), -1)
    rank = jnp.einsum("ts,bse->bte", before, blocks, preferred_element_type=F32)
    rank = rank + (CAPACITY * (jnp.arange(owners) % 2)).astype(F32)[:, None, None]
    place = jnp.where(blocks > 0, rank, -1.0).astype(jnp.int32).reshape(owners * rows, local)
    gate_here = lax.dynamic_slice(
        all_rows, (0, width + first_expert), (all_rows.shape[0], local)
    ).astype(F32) + lax.dynamic_slice(
        all_rows, (0, width + expert_count + first_expert), (all_rows.shape[0], local)
    ).astype(F32)
    lane = jnp.arange(128, dtype=jnp.int32)[None, :]
    starts = jnp.arange(2 * local, dtype=jnp.int32)
    wanted = first_expert + starts // 2 + expert_count * (starts % 2)
    lanes = (lane == wanted[:, None]).astype(F32)
    out_terms, back_terms, gate_grad, up_grad, down_grad = experts(
        all_rows, all_grads, place.T, place, gate_here.T, lanes, gate_weight, up_weight, down_weight
    )
    back_sum = plane_scatter(back_terms, 5)
    out_sum = plane_scatter(out_terms, 6)
    experts_out, back_total = tensor_sum([out_sum, back_sum], 7)
    output = hidden_state + experts_out.astype(F32)

    grad_out = cotangent.astype(F32)
    shares = back_total[:, width : width + expert_count].astype(F32)
    shares = shares + back_total[:, width + expert_count :].astype(F32)
    grad_logits = (shares - gates * jnp.sum(shares, axis=-1, keepdims=True)).astype(BF16)
    router_grad = matmul(routed_low, grad_logits, ((0,), (0,)))
    grad_routed = back_total[:, :width].astype(F32) + matmul(grad_logits, router, ((1,), (1,)))
    grad_hidden_norm, second_gain_grad = rms_back(
        hidden_state, second_inverse, second_gain, grad_routed
    )
    grad_hidden = grad_out + grad_hidden_norm
    grad_mixed = grad_hidden.astype(BF16)
    output_grad = matmul(grad_mixed, attended_low, ((0,), (0,)))
    grad_attended = matmul(grad_mixed, output_turned).astype(BF16).reshape(rows, heads, head)
    raw_again = jnp.einsum("bgd,ld->bgl", query_low, all_keys, preferred_element_type=F32)
    probabilities = jnp.exp(jnp.where(allowed, raw_again * scale, -1e30) - log_total)
    grad_probs = jnp.einsum("bgd,ld->bgl", grad_attended, all_values, preferred_element_type=F32)
    row_delta = jnp.sum(probabilities * grad_probs, axis=-1, keepdims=True)
    grad_raw = (scale * probabilities * (grad_probs - row_delta)).astype(BF16)
    grad_query = jnp.einsum("bgl,ld->bgd", grad_raw, all_keys, preferred_element_type=F32)
    grad_keys_all = jnp.einsum("bgl,bgd->ld", grad_raw, query_low, preferred_element_type=F32)
    grad_values_all = jnp.einsum(
        "bgl,bgd->ld", probabilities.astype(BF16), grad_attended, preferred_element_type=F32
    )
    grad_both = context_scatter(jnp.concatenate([grad_keys_all, grad_values_all], axis=1), 8)
    grad_keys = grad_both[:, :head].reshape(rows, 1, head)
    grad_values = grad_both[:, head:]
    grad_query_raw, query_gain_part = rms_back(
        query_unrotated,
        query_inverse,
        query_gain_wide,
        rotate_back(grad_query, cosine_table, sine_table),
    )
    grad_key_raw, key_gain_part = rms_back(
        key_unrotated, key_inverse, key_gain_wide, rotate_back(grad_keys, cosine_table, sine_table)
    )
    grad_qkv = jnp.concatenate(
        [
            grad_query_raw.astype(BF16).reshape(rows, query_columns),
            grad_key_raw.astype(BF16).reshape(rows, key_columns),
            grad_values.astype(BF16),
        ],
        axis=1,
    )
    qkv_grad = matmul(normed_low, grad_qkv, ((0,), (0,)))
    grad_normed_part = matmul(grad_qkv, qkv_matrix, ((1,), (1,)))
    gain_parts = jnp.pad(jnp.stack([query_gain_part, key_gain_part]), ((0, rows - 2), (0, 0)))
    (normed_total,) = tensor_sum([jnp.concatenate([grad_normed_part, gain_parts], axis=1)], 9)
    grad_normed = normed_total[:, :width].astype(F32)
    head_gains = normed_total[:2, width:].astype(F32)
    grad_tokens_norm, first_gain_grad = rms_back(residual, first_inverse, first_gain, grad_normed)
    tokens_grad = grad_hidden + grad_tokens_norm

    def spread(vector):
        each = vector.shape[0] // owners
        return jnp.pad(vector.reshape(owners, each), ((0, 0), (0, shard - each))).reshape(-1, 1)

    terms = jnp.concatenate(
        [
            qkv_grad,
            output_grad,
            router_grad,
            first_gain_grad[:, None],
            second_gain_grad[:, None],
            spread(head_gains[0]),
            spread(head_gains[1]),
            jnp.zeros((width, 128 - expert_count - 4), F32),
        ],
        axis=1,
    ).astype(BF16)
    total = plane_scatter(terms, 10)
    after = qkv_columns + query_columns
    few = head // owners
    return (
        output[None],
        tokens_grad[None],
        total[:, after + expert_count],
        total[:, :query_columns],
        total[:, query_columns : query_columns + key_columns],
        total[:, query_columns + key_columns : qkv_columns],
        total[:few, after + expert_count + 2],
        total[:few, after + expert_count + 3],
        total[:, qkv_columns:after].T,
        total[:, after + expert_count + 1],
        total[:, after : after + expert_count],
        gate_grad,
        up_grad,
        down_grad,
    )


def solution(mesh):
    plane_rows = P(PLANE)
    both = P(PLANE, "tensor")
    tokens = P("dp", "context", None)
    expert_rows = P(PLANE, "tensor", None)
    router = P(PLANE, None)
    output_matrix = P("tensor", PLANE)
    return jax.shard_map(
        per_device,
        mesh=mesh,
        in_specs=(
            tokens, tokens, plane_rows, both, both, both, P(), P(), output_matrix, plane_rows,
            router, expert_rows, expert_rows, expert_rows, tokens,
        ),
        out_specs=(
            tokens, tokens, plane_rows, both, both, both, plane_rows, plane_rows, output_matrix,
            plane_rows, router, expert_rows, expert_rows, expert_rows,
        ),
        check_vma=False,
    )
```

time: 1500 us -> 551 us (0.37)
  waiting for transfers between devices: 693 us -> 0 us
  Pallas kernels: 0 us -> 423 us
  blocking collectives: 421 us -> 0 us
  matrix products: 120 us -> 32.2 us
  other arithmetic: 85 us -> 16.5 us
  starting transfers between devices: 60 us -> 0 us
  local copies, waits for them, and re-layouts: 97.3 us -> 69.2 us
  between operations: 17.5 us -> 2.05 us
    pallas_call x0 -> x12, Pallas kernels: none -> 423 us  [the longest x3 145 us: plane_gather(): pl.pallas_call(functools.partial(gather_body, count), out_shape=[jax.Shap...]
    reduce_scatter x7 -> x0, waiting for transfers between devices: 333 us -> none  [the longest x1 96.7 us: per_device(): lax.psum_scatter(query_grad, ('dp', 'context'), scatter_dimension=0, tile...]
    all_to_all x4 -> x0, waiting for transfers between devices: 252 us -> none  [the longest x1 93.8 us: per_device(): lax.all_to_all(grad_outgoing, ('dp', 'context'), split_axis=0, concat_axi...]
    all_gather x5 -> x0, blocking collectives: 215 us -> none  [the longest x1 139 us: per_device(): lax.all_gather(router_matrix, ('dp', 'context'), axis=0, tiled=True)]
    unnamed x2 -> x0, blocking collectives: 190 us -> none
    psum x3 -> x0, waiting for transfers between devices: 106 us -> none  [the longest x1 54.9 us: per_device(): lax.psum((grad_routed_part, grad_gates_part), 'tensor')]
    dot_general x30 -> x16, matrix products: 120 us -> 32.2 us  [the longest x9 23.5 us: matmul(): lax.dot_general(a, b, (contract, ((), ())), preferred_element_type=F32)]
    all_to_all x4 -> x0, starting transfers between devices: 59 us -> none  [the longest x1 22 us: per_device(): lax.all_to_all(expert_rows, ('dp', 'context'), split_axis=0, concat_axis=...]
  transfers between devices with their start and end apart: 16 -> 0, of which waited for: 12 -> 0; matrix products, arithmetic and copies ran while one was open for 14% -> 0% of each run, Pallas kernels for 0% -> 0%
where the time goes in v1:
time: 551 us; the launch traced here: 543 us
  Pallas kernels  423 us (77%)
  local copies, waits for them, and re-layouts  69.2 us (13%)
  matrix products  32.2 us (6%)
  other arithmetic  16.5 us (3%)
    pallas_call x3, Pallas kernels, plane_gather(): pl.pallas_call(functools.partial(gather_body, count), out_shape=[jax.Shap...  145 us
    pallas_call x3, Pallas kernels, plane_scatter(): pl.pallas_call(functools.partial(scatter_body, rows), out_shape=jax.Shape...  141 us
    pallas_call x3, Pallas kernels, tensor_sum(): pl.pallas_call(functools.partial(tensor_sum_body, count), out_shape=[jax....  54.4 us
    pallas_call x1, Pallas kernels, experts(): pl.pallas_call(functools.partial(experts_body, steps, width), grid=(steps...  50.4 us
    unnamed x95, local copies, waits for them, and re-layouts  33.7 us
    dot_general x9, matrix products, matmul(): lax.dot_general(a, b, (contract, ((), ())), preferred_element_type=F32)  23.5 us
    pallas_call x1, Pallas kernels, context_scatter(): pl.pallas_call(context_scatter_body, out_shape=jax.ShapeDtypeStruct((rows...  20.1 us
    concatenate x1, local copies, waits for them, and re-layouts, per_device(): jnp.concatenate([qkv_grad, output_grad, router_grad, first_gain_grad[:, N...  17.2 us

profile of v1, /device:TPU:1, one launch (start us, length us, event | category | flops | bytes accessed | tf_op | source)
XLA Modules:
  0.0 543.3 jit_solution(1093955829760883421)
XLA Ops:
  0.6 0.8 copy.182
  1.4 0.8 copy.183
  2.2 1.1 concatenate.53.refs_0_
  3.3 36.9 %shard_map.254 = bf16[2048,2432]{1,0:T(8,128)(2,1)S(1)} custom-call(bf16[64,2432]{1,0:T(8,128)(2,1)S(1)} %concatenate.53.refs_0_), custom_call_target="tpu_custom_call" | custom-call | tf_op jit(solution)/shard_map/pallas_call | solution.py:186
  40.2 0.7 convert_reduce_fusion
  41.1 0.5 multiply_multiply_fusion.1
  41.6 2.3 copy-done.5
  43.9 0.9 fusion.2
  45.0 0.6 multiply_multiply_fusion.2
  46.1 0.7 pad_maximum_fusion.8.mine
  46.8 11.9 %shard_map.255 = bf16[1024,256]{1,0:T(8,128)(2,1)} custom-call(bf16[128,256]{1,0:T(8,128)(2,1)} %pad_maximum_fusion.8.mine), custom_call_target="tpu_custom_call" | custom-call | tf_op jit(solution)/shard_map/pallas_call | solution.py:466
  59.4 0.9 fusion.84
  60.8 1.0 fusion.102
  61.9 1.1 fusion.4
  63.0 1.2 fusion.21
  64.2 0.7 copy-done.26
  64.9 3.7 fusion.7.refs_0_
  68.7 17.0 %shard_map.256 = bf16[128,2048]{1,0:T(8,128)(2,1)S(1)} custom-call(f32[128,2048]{1,0:T(8,128)S(1)} %fusion.7.refs_0_), custom_call_target="tpu_custom_call" | custom-call | tf_op jit(solution)/shard_map/pallas_call | solution.py:423
  85.9 0.5 multiply_multiply_fusion.3
  87.1 1.4 fusion.103
  89.1 55.0 %shard_map.257.x_ref = bf16[4096,2176]{1,0:T(8,128)(2,1)S(1)} custom-call(bf16[128,2176]{1,0:T(8,128)(2,1)S(1)} %concatenate.58.refs_0_), custom_call_target="tpu_custom_call" | custom-call | tf_op jit(solution)/shard_map/pallas_call | solution.py:186
  144.2 6.1 %copy-done.1 = bf16[4096,2176]{1,0:T(8,128)(2,1)} copy-done((bf16[4096,2176]{1,0:T(8,128)(2,1)}, bf16[4096,2176]{1,0:T(8,128)(2,1)S(1)}, u32[]{:S(2)}) %copy-start.1) | copy-done | bytes 17825816
  150.3 2.3 constant_dynamic-slice_fusion.1
  153.4 0.6 add_bitcast_fusion.1.gate_ref
  154.1 1.1 pad_maximum_fusion.2.refs_0_
  155.2 53.4 %shard_map.258.c_ref = bf16[4096,2176]{1,0:T(8,128)(2,1)S(1)} custom-call(bf16[128,2176]{1,0:T(8,128)(2,1)S(1)} %pad_maximum_fusion.2.refs_0_), custom_call_target="tpu_custom_call" | custom-call | tf_op jit(solution)/shard_map/pallas_call | solution.py:186
  208.5 6.1 %copy-done.2 = bf16[4096,2176]{1,0:T(8,128)(2,1)} copy-done((bf16[4096,2176]{1,0:T(8,128)(2,1)}, bf16[4096,2176]{1,0:T(8,128)(2,1)S(1)}, u32[]{:S(2)}) %copy-start.2) | copy-done | bytes 17825816
  215.6 0.7 copy.192
  216.3 1.4 copy-done.12
  217.6 1.2 copy.195.row_ref
  218.9 0.7 fusion.87.lane_ref
  219.5 50.4 %shard_map.259 = (bf16[4096,2048]{1,0:T(8,128)(2,1)}, bf16[4096,2176]{1,0:T(8,128)(2,1)}, f32[2,192,2048]{2,1,0:T(8,128)}, f32[2,192,2048]{2,1,0:T(8,128)}, f32[2,192,2048]{2,1,0:T(8,128)}) custom-call(bf16[4096,2176]{1,0:T(8,128)(2,1)} %copy-done.1, bf16[4096,2176]{1,0:T(8,128)(2,1)} %copy-done.2, s32[2,4096]{1,0:T(2,128)} %copy.195.row_ref, ...), custom_call_target="tpu_custom_call" | custom-call | flops 23085449216 | bytes 83886080 | tf_op jit(solution)/shard_map/pallas_call | solution.py:628
  269.9 6.1 %copy-done.3 = bf16[4096,2176]{1,0:T(8,128)(2,1)S(1)} copy-done((bf16[4096,2176]{1,0:T(8,128)(2,1)S(1)}, bf16[4096,2176]{1,0:T(8,128)(2,1)}, u32[]{:S(2)}) %copy-start.3) | copy-done | bytes 17825816
  276.0 54.4 %shard_map.261.refs_1_ = f32[128,2176]{1,0:T(8,128)S(1)} custom-call(bf16[4096,2176]{1,0:T(8,128)(2,1)S(1)} %copy-done.3), custom_call_target="tpu_custom_call" | custom-call | tf_op jit(solution)/shard_map/pallas_call | solution.py:333
  330.4 5.8 %copy-done.4 = bf16[4096,2048]{1,0:T(8,128)(2,1)S(1)} copy-done((bf16[4096,2048]{1,0:T(8,128)(2,1)S(1)}, bf16[4096,2048]{1,0:T(8,128)(2,1)}, u32[]{:S(2)}) %copy-start.4) | copy-done | bytes 16777240
  336.2 51.9 %shard_map.260.refs_0_ = f32[128,2048]{1,0:T(8,128)S(1)} custom-call(bf16[4096,2048]{1,0:T(8,128)(2,1)S(1)} %copy-done.4), custom_call_target="tpu_custom_call" | custom-call | tf_op jit(solution)/shard_map/pallas_call | solution.py:333
  388.0 19.9 %shard_map.262 = (bf16[128,2048]{1,0:T(8,128)(2,1)S(1)}, bf16[128,2176]{1,0:T(8,128)(2,1)S(1)}) custom-call(f32[128,2048]{1,0:T(8,128)S(1)} %shard_map.260.refs_0_, f32[128,2176]{1,0:T(8,128)S(1)} %shard_map.261.refs_1_), custom_call_target="tpu_custom_call" | custom-call | tf_op jit(solution)/shard_map/pallas_call | solution.py:423
  408.5 1.0 copy.211
  409.6 2.5 multiply_reduce_fusion.1
  412.1 1.4 subtract_add_fusion
  413.5 3.3 convolution_convert_fusion.1
  416.8 3.0 fusion.18
  420.0 3.6 multiply_reduce_fusion
  423.7 1.4 multiply_convert_fusion
  425.1 0.9 convolution_bitcast_fusion
  426.0 1.0 fusion.15
  427.2 20.1 %shard_map.263 = f32[128,256]{1,0:T(8,128)S(1)} custom-call(f32[1024,256]{1,0:T(8,128)S(1)} %pad_maximum_fusion.1.part), custom_call_target="tpu_custom_call" | custom-call | tf_op jit(solution)/shard_map/pallas_call | solution.py:504
  448.0 0.7 fusion.45
  450.8 4.0 convolution_convert_fusion
  454.8 4.3 fusion
  459.2 17.6 %shard_map.264 = bf16[128,2176]{1,0:T(8,128)(2,1)S(1)} custom-call(f32[128,2176]{1,0:T(8,128)S(1)} %pad_maximum_fusion.refs_0_), custom_call_target="tpu_custom_call" | custom-call | tf_op jit(solution)/shard_map/pallas_call | solution.py:423
  476.9 1.1 reshape.437
  478.2 1.1 reshape.438
  480.0 1.2 broadcast_in_dim.109
  481.1 0.9 broadcast_in_dim.107
  482.0 17.2 %concatenate.68.part_ref = bf16[2048,2432]{1,0:T(8,128)(2,1)} concatenate(bf16[2048,1280]{1,0:T(8,128)(2,1)} %convolution_convert_fusion, bf16[2048,1024]{1,0:T(8,128)(2,1)} %convolution_convert_fusion.1, bf16[2048,64]{1,0:T(8,128)(2,1)S(1)} %copy-done.24, bf16[2048,1]{1,0:T(8,128)(2,1)S(1)} %broadcast_in_dim.108, bf16[2048,1]{1,0:T(8,128)(2,1)} %broadcast_in_dim.109, ...), dimensions={1} | concatenate | bytes 19922944 | tf_op jit(solution)/shard_map/concatenate | solution.py:881
  499.2 3.8 copy-done
  503.0 34.9 %shard_map.265 = f32[64,2432]{1,0:T(8,128)S(1)} custom-call(bf16[2048,2432]{1,0:T(8,128)(2,1)S(1)} %copy-done), custom_call_target="tpu_custom_call" | custom-call | tf_op jit(solution)/shard_map/pallas_call | solution.py:333
  537.9 0.8 slice_bitcast_fusion.2
  538.7 0.6 fusion.101
  539.4 0.6 slice.150
  540.0 0.7 slice_reduce_fusion
  540.7 0.7 slice_reduce_fusion.2
  541.4 1.4 fusion.27
  (150 shorter events, 9.6 us)
Async XLA Ops:
  3.3 37.6 %copy-start.8 = (bf16[1,128,2048]{2,1,0:T(8,128)(2,1)S(1)}, bf16[1,128,2048]{2,1,0:T(8,128)(2,1)}, u32[]{:S(2)}) copy-start(bf16[1,128,2048]{2,1,0:T(8,128)(2,1)} %param.15) | copy-start | bytes 1572868
  40.2 3.7 copy-start.5
  41.1 4.5 copy-start.43
  44.9 17.0 %copy-start.19 = (f32[128,1280]{1,0:T(8,128)}, f32[128,1280]{1,0:T(8,128)S(1)}, u32[]{:S(2)}) copy-start(f32[128,1280]{1,0:T(8,128)S(1)} %fusion.2) | copy-start | bytes 1966084
  44.9 14.3 %copy-start.44 = (bf16[128]{0:T(256)(128)(2,1)S(1)}, bf16[128]{0:T(256)(128)(2,1)}, u32[]{:S(2)}) copy-start(bf16[128]{0:T(256)(128)(2,1)} %param.21) | copy-start | bytes 772
  45.7 16.2 %copy-start.28 = (f32[64]{0:T(128)}, f32[64]{0:T(128)S(1)}, u32[]{:S(2)}) copy-start(f32[64]{0:T(128)S(1)} %multiply_exponential_fusion) | copy-start | bytes 772
  58.7 2.1 copy-start.17
  58.8 3.1 copy-start.13
  59.2 1.4 copy-start.30
  60.6 2.4 copy-start.21
  61.9 2.3 copy-start.6
  64.2 0.7 copy-start.26
  64.9 22.0 %copy-start.37 = (s32[1,128,8]{1,2,0:T(8,128)S(1)}, s32[1,128,8]{1,2,0:T(8,128)}, u32[]{:S(2)}) copy-start(s32[1,128,8]{1,2,0:T(8,128)} %param.16) | copy-start | bytes 12292
  86.5 0.5 copy-start.38
  86.7 57.5 %copy-start.15 = (bf16[128,2048]{1,0:T(8,128)(2,1)}, bf16[128,2048]{1,0:T(8,128)(2,1)S(1)}, u32[]{:S(2)}) copy-start(bf16[128,2048]{1,0:T(8,128)(2,1)S(1)} %multiply_convert_fusion.1) | copy-start | bytes 1572868
  88.5 55.6 %copy-start.32 = (f32[128]{0:T(128)}, f32[128]{0:T(128)S(1)}, u32[]{:S(2)}) copy-start(f32[128]{0:T(128)S(1)} %get-tuple-element.79) | copy-start | bytes 1540
  88.7 55.5 %copy-start.34 = (f32[128]{0:T(128)}, f32[128]{0:T(128)S(1)}, u32[]{:S(2)}) copy-start(f32[128]{0:T(128)S(1)} %fusion.78) | copy-start | bytes 1540
  144.2 6.1 %copy-start.1 = (bf16[4096,2176]{1,0:T(8,128)(2,1)}, bf16[4096,2176]{1,0:T(8,128)(2,1)S(1)}, u32[]{:S(2)}) copy-start(bf16[4096,2176]{1,0:T(8,128)(2,1)S(1)} %shard_map.257.x_ref) | copy-start | bytes 53477380
  208.5 6.1 %copy-start.2 = (bf16[4096,2176]{1,0:T(8,128)(2,1)}, bf16[4096,2176]{1,0:T(8,128)(2,1)S(1)}, u32[]{:S(2)}) copy-start(bf16[4096,2176]{1,0:T(8,128)(2,1)S(1)} %shard_map.258.c_ref) | copy-start | bytes 53477380
  216.3 1.4 copy-start.12
  269.9 6.1 %copy-start.3 = (bf16[4096,2176]{1,0:T(8,128)(2,1)S(1)}, bf16[4096,2176]{1,0:T(8,128)(2,1)}, u32[]{:S(2)}) copy-start(bf16[4096,2176]{1,0:T(8,128)(2,1)} %get-tuple-element.22.part_ref) | copy-start | bytes 53477380
  330.4 5.8 %copy-start.4 = (bf16[4096,2048]{1,0:T(8,128)(2,1)S(1)}, bf16[4096,2048]{1,0:T(8,128)(2,1)}, u32[]{:S(2)}) copy-start(bf16[4096,2048]{1,0:T(8,128)(2,1)} %get-tuple-element.21.part_ref) | copy-start | bytes 50331652
  336.1 72.0 %copy-start.16 = (bf16[128,2048]{1,0:T(8,128)(2,1)S(1)}, bf16[128,2048]{1,0:T(8,128)(2,1)}, u32[]{:S(2)}) copy-start(bf16[128,2048]{1,0:T(8,128)(2,1)} %copy-done.15) | copy-start | bytes 1572868
  336.1 72.0 %copy-start.33 = (f32[128]{0:T(128)S(1)}, f32[128]{0:T(128)}, u32[]{:S(2)}) copy-start(f32[128]{0:T(128)} %copy-done.32) | copy-start | bytes 1540
  336.1 72.0 %copy-start.35 = (f32[128]{0:T(128)S(1)}, f32[128]{0:T(128)}, u32[]{:S(2)}) copy-start(f32[128]{0:T(128)} %copy-done.34) | copy-start | bytes 1540
  336.1 73.4 %copy-start.39 = (f32[128]{0:T(128)S(1)}, f32[128]{0:T(128)}, u32[]{:S(2)}) copy-start(f32[128]{0:T(128)} %copy-done.38) | copy-start | bytes 1540
  388.0 24.0 %copy-start.42 = (f32[128]{0:T(128)S(1)}, f32[128]{0:T(128)}, u32[]{:S(2)}) copy-start(f32[128]{0:T(128)} %get-tuple-element.75) | copy-start | bytes 1540
  407.9 4.1 copy-start.9
  407.9 4.1 copy-start.23
  409.6 4.0 copy-start.27
  413.5 3.3 copy-start.10
  416.8 3.2 copy-start.18
  420.0 3.7 copy-start.7
  423.7 1.4 copy-start.22
  426.0 21.3 %copy-start.29 = (f32[64]{0:T(128)S(1)}, f32[64]{0:T(128)}, u32[]{:S(2)}) copy-start(f32[64]{0:T(128)} %copy-done.28) | copy-start | bytes 772
  426.0 21.7 %copy-start.20 = (f32[128,1280]{1,0:T(8,128)S(1)}, f32[128,1280]{1,0:T(8,128)}, u32[]{:S(2)}) copy-start(f32[128,1280]{1,0:T(8,128)} %copy-done.19) | copy-start | bytes 1966084
  426.0 21.8 %copy-start.41 = (f32[128]{0:T(128)S(1)}, f32[128]{0:T(128)}, u32[]{:S(2)}) copy-start(f32[128]{0:T(128)} %get-tuple-element.73) | copy-start | bytes 1540
  427.1 21.7 %copy-start.25 = (f32[128,64]{1,0:T(8,128)S(1)}, f32[128,64]{1,0:T(8,128)}, u32[]{:S(2)}) copy-start(f32[128,64]{1,0:T(8,128)} %get-tuple-element.68) | copy-start | bytes 98308
  427.1 21.9 %copy-start.14 = (f32[16,8,8,128]{3,2,1,0:T(8,128)S(1)}, f32[16,8,8,128]{3,2,1,0:T(8,128)}, u32[]{:S(2)}) copy-start(f32[16,8,8,128]{3,2,1,0:T(8,128)} %copy-done.13) | copy-start | bytes 1572868
  427.1 21.9 %copy-start.31 = (f32[128]{0:T(128)S(1)}, f32[128]{0:T(128)}, u32[]{:S(2)}) copy-start(f32[128]{0:T(128)} %copy-done.30) | copy-start | bytes 1540
  459.1 20.9 %copy-start.36 = (bf16[2048]{0:T(1024)(128)(2,1)S(1)}, bf16[2048]{0:T(1024)(128)(2,1)}, u32[]{:S(2)}) copy-start(bf16[2048]{0:T(1024)(128)(2,1)} %get-tuple-element.30) | copy-start | bytes 12292
  459.1 22.9 %copy-start.24 = (bf16[2048,64]{1,0:T(8,128)(2,1)S(1)}, bf16[2048,64]{1,0:T(8,128)(2,1)}, u32[]{:S(2)}) copy-start(bf16[2048,64]{1,0:T(8,128)(2,1)} %copy.211) | copy-start | bytes 786436
  499.2 3.8 copy-start
  503.0 38.4 %copy-start.11 = (f32[128,2048]{1,0:T(8,128)S(1)}, f32[128,2048]{1,0:T(8,128)}, u32[]{:S(2)}) copy-start(f32[128,2048]{1,0:T(8,128)} %copy-done.10) | copy-start | bytes 3145732
  503.0 38.4 %copy-start.40 = (f32[128]{0:T(128)S(1)}, f32[128]{0:T(128)}, u32[]{:S(2)}) copy-start(f32[128]{0:T(128)} %get-tuple-element.71) | copy-start | bytes 1540
